TPU v7x, 128 devices: a whole 4x4x4 slice. The times are simulated.
128 devices in a mesh: lat: 4 (over z), lon: 32 (over x, y, core).
Axes of the slice: x: 4, y: 4, z: 4, core: 2. Of those that a mesh axis runs over, the one named last changes fastest.
Arguments:
- latent: bfloat16 [4096, 64, 512], P(('lat', 'lon')), may hold values from -6 to 6
- patch_owner: int32 [12288, 2], P(('lat', 'lon')), may hold values from 0 to 127, all different within a row; in each aligned block of 96 rows (0 to 95, 96 to 191, ...) at most 2 rows name the same one
- patch_local: int32 [12288, 2], P(('lat', 'lon')), may hold values from 0 to 31
- obs_patch: int32 [12288, 128], P(('lat', 'lon')), may hold values from 0 to 1
- cell_offset: int32 [12288, 128], P(('lat', 'lon')), may hold values from 0 to 48
- frac: float32 [12288, 2, 128], P(('lat', 'lon')), may hold values from 0 to 1
- obs_value: float32 [12288, 128], P(('lat', 'lon')), may hold values from -6 to 6
- obs_weight: float32 [12288, 128], P(('lat', 'lon')), may hold values from 0.5 to 4
- w_hidden: bfloat16 [256, 256], replicated, may hold values from -0.375 to 0.375
- b_hidden: float32 [256], replicated, may hold values from -3 to 3
- w_out: bfloat16 [256], replicated, may hold values from -0.375 to 0.375
Outputs:
- latent_grad: float32 [4096, 64, 512], P(('lat', 'lon'))
- obs_score: float32 [12288, 128], P(('lat', 'lon'))
Inputs may be any that keep to these rules, and one draw needn't show every extreme that they name: `patch_owner`: the 2 entries of a block name different devices; among the 96 blocks of one device no device is named more than 2 times, and some device exactly 2 times.
All inputs are finite; a program needn't handle non-finite values.
Results may differ from a plain program's by a relative error of at most 0.006.
Values may be sent and summed in bfloat16 or wider, within the bound.
A program may use at most 128 MiB of HBM per device.

v0:
```python
import math

import jax
import jax.numpy as jnp
from jax import lax
from jax.sharding import PartitionSpec as P

root_coef = 0.7978845608028654
cubic_coef = 0.044715
smooth_sq = 0.01
loss_scale = 64.0


def gelu_pair(pre_act):
    inner_arg = root_coef * (pre_act + cubic_coef * pre_act * pre_act * pre_act)
    tangent = jnp.tanh(inner_arg)
    result = 0.5 * pre_act * (1.0 + tangent)
    derivative = 0.5 * (1.0 + tangent) + 0.5 * pre_act * (1.0 - tangent * tangent) * root_coef * (
        1.0 + 3.0 * cubic_coef * pre_act * pre_act
    )
    return (result, derivative)


def decode(sampled, w_hidden, b_hidden, w_out, obs_vals, obs_wts):
    n_rows = sampled.shape[0]
    n_chan = w_hidden.shape[0]
    inputs = sampled.reshape(n_rows * 2, n_chan)
    pre_act = jnp.dot(inputs, w_hidden, preferred_element_type=jnp.float32) + b_hidden
    activ, derivative = gelu_pair(pre_act)
    activ = activ.astype(jnp.bfloat16)
    predicted = jnp.dot(activ, w_out, preferred_element_type=jnp.float32).reshape(n_rows, 2)
    member_one = predicted[:, 0]
    member_two = predicted[:, 1]
    err_one = member_one - obs_vals
    err_two = member_two - obs_vals
    between = member_one - member_two
    soft_one = jnp.sqrt(err_one * err_one + smooth_sq)
    soft_two = jnp.sqrt(err_two * err_two + smooth_sq)
    soft_mid = jnp.sqrt(between * between + smooth_sq)
    penalty = obs_wts * (0.5 * (soft_one + soft_two) - 0.5 * soft_mid)
    scaled = 0.5 * loss_scale * obs_wts
    grad_one = scaled * (err_one / soft_one - between / soft_mid)
    grad_two = scaled * (err_two / soft_two + between / soft_mid)
    grad_pred = jnp.stack([grad_one, grad_two], axis=1).reshape(n_rows * 2)
    delta = (grad_pred[:, None] * w_out.astype(jnp.float32)[None, :] * derivative).astype(
        jnp.bfloat16
    )
    back_grad = jnp.dot(delta, w_hidden.T, preferred_element_type=jnp.float32).reshape(
        n_rows, 2 * n_chan
    )
    return (penalty, back_grad.astype(jnp.bfloat16))


def corner_matrix(offsets, entry, frac_lat, frac_lon, n_cols):
    row_part = offsets // 7
    col_part = offsets % 7
    corner = (entry * 64 + row_part * 8 + col_part)[..., None]
    columns = lax.broadcasted_iota(jnp.int32, offsets.shape + (n_cols,), offsets.ndim)
    lat_part = frac_lat[..., None]
    lon_part = frac_lon[..., None]
    matrix = jnp.where(columns == corner, (1.0 - lat_part) * (1.0 - lon_part), 0.0)
    matrix = matrix + jnp.where(columns == corner + 1, (1.0 - lat_part) * lon_part, 0.0)
    matrix = matrix + jnp.where(columns == corner + 8, lat_part * (1.0 - lon_part), 0.0)
    matrix = matrix + jnp.where(columns == corner + 9, lat_part * lon_part, 0.0)
    return matrix


def interpolate_and_decode(matrix, patch_rows, w_hidden, b_hidden, w_out, obs_vals, obs_wts):
    n_group, n_obs, _ = matrix.shape
    n_cols = patch_rows.shape[2]
    weights = matrix.astype(jnp.bfloat16)
    sampled = jnp.einsum(
        "goj,gjc->goc", weights, patch_rows, preferred_element_type=jnp.float32
    ).astype(jnp.bfloat16)
    penalty, back_grad = decode(
        sampled.reshape(n_group * n_obs, n_cols),
        w_hidden,
        b_hidden,
        w_out,
        obs_vals.reshape(n_group * n_obs),
        obs_wts.reshape(n_group * n_obs),
    )
    back_grad = back_grad.reshape(n_group, n_obs, n_cols)
    spread = jnp.einsum(
        "goj,goc->gjc", weights, back_grad, preferred_element_type=jnp.float32
    ).astype(jnp.bfloat16)
    return (penalty.reshape(n_group, n_obs), spread)


def per_device(
    latent,
    patch_owner,
    patch_local,
    obs_patch,
    cell_offset,
    frac,
    obs_value,
    obs_weight,
    w_hidden,
    b_hidden,
    w_out,
):
    devices = lax.axis_size(("lat", "lon"))
    blocks, entries = patch_owner.shape
    per_block = obs_patch.shape[1]
    n_patches, n_cells, columns_all = latent.shape
    requests = blocks * entries
    capacity = max(2, 3 * requests // (2 * devices))
    n_slots = devices * capacity
    owners = patch_owner.reshape(requests)
    owner_table = (owners[:, None] == jnp.arange(devices, dtype=jnp.int32)[None, :]).astype(
        jnp.int32
    )
    earlier = jnp.cumsum(owner_table, axis=0) - owner_table
    slot_rank = jnp.sum(earlier * owner_table, axis=1)
    slot_of = owners * capacity + slot_rank
    local_ids = patch_local.reshape(requests)
    patch_iota = jnp.arange(n_patches, dtype=jnp.int32)
    wanted = jnp.full((n_slots,), -1, jnp.int32).at[slot_of].set(local_ids)
    asked_ids = lax.all_to_all(wanted, ("lat", "lon"), split_axis=0, concat_axis=0, tiled=True)
    served = jnp.take(latent, jnp.maximum(asked_ids, 0), axis=0)
    arrived = lax.all_to_all(served, ("lat", "lon"), split_axis=0, concat_axis=0, tiled=True)
    per_group = math.gcd(blocks, 8)
    rounds = blocks // per_group

    def one_group(inputs):
        slot_group, entry_g, offset_g, frac_g, value_g, weight_g = inputs
        patch_rows = jnp.take(arrived, slot_group.reshape(per_group * entries), axis=0)
        patch_rows = patch_rows.reshape(per_group, entries * n_cells, columns_all)
        matrix = corner_matrix(
            offset_g, entry_g, frac_g[:, 0, :], frac_g[:, 1, :], entries * n_cells
        )
        penalty, spread = interpolate_and_decode(
            matrix, patch_rows, w_hidden, b_hidden, w_out, value_g, weight_g
        )
        return (penalty, spread.reshape(per_group * entries, n_cells, columns_all))

    packed = (
        slot_of.reshape(rounds, per_group, entries),
        obs_patch.reshape(rounds, per_group, per_block),
        cell_offset.reshape(rounds, per_group, per_block),
        frac.reshape(rounds, per_group, 2, per_block),
        obs_value.reshape(rounds, per_group, per_block),
        obs_weight.reshape(rounds, per_group, per_block),
    )
    scores, pieces = lax.map(one_group, packed)
    outgoing = (
        jnp.zeros((n_slots, n_cells, columns_all), jnp.bfloat16)
        .at[slot_of]
        .set(pieces.reshape(requests, n_cells, columns_all))
    )
    returned = lax.all_to_all(outgoing, ("lat", "lon"), split_axis=0, concat_axis=0, tiled=True)
    onehot = (asked_ids[None, :] == patch_iota[:, None]).astype(jnp.bfloat16)
    summed = jnp.dot(
        onehot, returned.reshape(n_slots, n_cells * columns_all), preferred_element_type=jnp.float32
    )
    latent_grad = summed.reshape(latent.shape)
    obs_score = scores.reshape(blocks, per_block)
    return (latent_grad, obs_score)


def solution(mesh):
    return jax.shard_map(
        per_device,
        mesh=mesh,
        in_specs=(
            P(("lat", "lon"), None, None),
            P(("lat", "lon"), None),
            P(("lat", "lon"), None),
            P(("lat", "lon"), None),
            P(("lat", "lon"), None),
            P(("lat", "lon"), None, None),
            P(("lat", "lon"), None),
            P(("lat", "lon"), None),
            P(),
            P(),
            P(),
        ),
        out_specs=(P(("lat", "lon"), None, None), P(("lat", "lon"), None)),
        check_vma=False,
    )
```

profile of v0, /device:TPU:1, one launch (start us, length us, event | category | flops | bytes accessed | tf_op | source)
XLA Modules:
  0.0 768.8 jit_solution(13950491515901954473)
XLA Ops:
  4.1 1.2 scatter_custom_fusion
  5.5 20.9 %all_to_all.19 = s32[128,2,1]{1,2,0:T(1,128)S(1)} all-to-all(s32[128,2,1]{1,2,0:T(1,128)S(1)} %bitcast.146), channel_id=1, replica_groups=mesh['lat'=4,'lon'=32] {'lat','lon'}, dimensions={0} | all-to-all | bytes 2048 | tf_op jit(solution)/shard_map/all_to_all | solution.py:120
  28.2 9.7 %gather_fusion.1 = bf16[256,64,512]{2,1,0:T(8,128)(2,1)} fusion(bf16[32,64,512]{2,1,0:T(8,128)(2,1)S(1)} %copy-done, s32[1024]{0:T(1024)S(1)} %pad_clamp_fusion.1), kind=kCustom, calls=%fused_computation.1 | custom fusion | bytes 33555456 | tf_op jit(solution)/shard_map/jit(_take)/gather | solution.py:121
  37.9 14.2 %broadcast_select_fusion = bf16[256,64,512]{2,1,0:T(8,128)(2,1)} fusion(bf16[256,64,512]{2,1,0:T(8,128)(2,1)} %gather_fusion.1, pred[256]{0:T(512)(128)(4,1)S(1)} %maximum_compare_fusion), kind=kLoop, calls=%fused_computation.74 | loop fusion | flops 8388608 | bytes 33554688 | tf_op jit(solution)/shard_map/jit(_take)/select_n | solution.py:121
  52.1 5.3 all-to-all-start.1
  57.5 217.6 %all-to-all-done.1 = bf16[256,64,512]{2,1,0:T(8,128)(2,1)} async-done(((bf16[256,64,512]{2,1,0:T(8,128)(2,1)}), bf16[256,64,512]{2,1,0:T(8,128)(2,1)}, u32[]{:S(2)}, u32[]{:S(2)}) %all-to-all-start.1) | async-done | bytes 16777248 | tf_op jit(solution)/shard_map/all_to_all | solution.py:122
  275.2 209.2 %while.14 = (s32[]{:T(128)}, f32[12,8,128]{2,1,0:T(8,128)S(1)}, bf16[12,16,64,512]{3,2,1,0:T(8,128)(2,1)}, f32[12,8,128]{2,1,0:T(8,128)}, s32[12,8,128]{2,1,0:T(...) while((s32[]{:T(128)}, f32[12,8,128]{2,1,0:T(8,128)S(1)}, ...), condition=%wide.region_5.6_spmd, body=%wide.region_4.5_spmd.sunk | while | flops 827387264 | bytes 40442316 | solution.py:146
  275.3 6.4 gather_fusion
  288.9 1.7 convolution_convert_fusion.7
  291.5 1.1 constant_dynamic-update-slice_fusion.2
  292.7 6.4 gather_fusion
  306.4 1.7 convolution_convert_fusion.7
  309.0 1.1 constant_dynamic-update-slice_fusion.2
  310.2 6.4 gather_fusion
  323.9 1.7 convolution_convert_fusion.7
  326.4 1.1 constant_dynamic-update-slice_fusion.2
  327.6 6.4 gather_fusion
  341.3 1.7 convolution_convert_fusion.7
  343.9 1.1 constant_dynamic-update-slice_fusion.2
  345.1 6.4 gather_fusion
  358.7 1.7 convolution_convert_fusion.7
  361.3 1.1 constant_dynamic-update-slice_fusion.2
  362.5 6.4 gather_fusion
  376.1 1.7 convolution_convert_fusion.7
  379.9 6.4 gather_fusion
  393.5 1.7 convolution_convert_fusion.7
  396.1 1.1 constant_dynamic-update-slice_fusion.2
  397.3 6.4 gather_fusion
  411.0 1.7 convolution_convert_fusion.7
  413.6 1.1 constant_dynamic-update-slice_fusion.2
  414.7 6.4 gather_fusion
  428.4 1.7 convolution_convert_fusion.7
  431.0 1.1 constant_dynamic-update-slice_fusion.2
  432.2 6.4 gather_fusion
  445.8 1.7 convolution_convert_fusion.7
  448.4 1.1 constant_dynamic-update-slice_fusion.2
  449.6 6.4 gather_fusion
  463.3 1.7 convolution_convert_fusion.7
  465.9 1.1 constant_dynamic-update-slice_fusion.2
  467.1 6.4 gather_fusion
  480.7 1.7 convolution_convert_fusion.7
  483.3 1.1 constant_dynamic-update-slice_fusion.2
  484.4 6.1 broadcast_in_dim.103
  490.5 34.8 %scatter_fusion = bf16[256,64,512]{2,1,0:T(8,128)(2,1)} fusion(bf16[256,64,512]{2,1,0:T(8,128)(2,1)} %broadcast_in_dim.103, s32[192]{0:T(256)S(1)} %bitcast.156, bf16[192,64,512]{2,1,0:T(8,128)(2,1)} %bitcast.136), kind=kCustom, calls=%fused_computation.3 | custom fusion | bytes 37749504 | tf_op jit(solution)/shard_map/scatter | solution.py:150
  525.3 199.2 %all_to_all.20 = bf16[256,64,512]{2,1,0:T(8,128)(2,1)} all-to-all(bf16[256,64,512]{2,1,0:T(8,128)(2,1)} %scatter_fusion), channel_id=1, replica_groups=mesh['lat'=4,'lon'=32] {'lat','lon'}, dimensions={0} | all-to-all | bytes 33554432 | tf_op jit(solution)/shard_map/all_to_all | solution.py:152
  724.5 25.0 %copy.107 = bf16[256,64,512]{0,2,1:T(8,128)(2,1)} copy(bf16[256,64,512]{2,1,0:T(8,128)(2,1)} %all_to_all.20) | data formatting | bytes 33554432 | tf_op jit(solution)/shard_map/reshape | solution.py:155
  749.5 12.5 %fusion.28 = f32[32,64,512]{2,0,1:T(8,128)} fusion(bf16[256,64,512]{0,2,1:T(8,128)(2,1)} %copy.107, s32[256]{0:T(256)S(1)} %eq.108), kind=kOutput, calls=%fused_computation.72 | convolution fusion | flops 536879104 | bytes 20972544 | tf_op jit(solution)/shard_map/dot_general | solution.py:154
  762.0 6.8 copy.103
  (474 shorter events, 103.5 us)
Async XLA Ops:
  0.6 27.6 %copy-start = (bf16[32,64,512]{2,1,0:T(8,128)(2,1)S(1)}, bf16[32,64,512]{2,1,0:T(8,128)(2,1)}, u32[]{:S(2)}) copy-start(bf16[32,64,512]{2,1,0:T(8,128)(2,1)} %param.13) | copy-start | bytes 6291460
  52.1 223.1 %copy-start.4 = (bf16[256,256]{1,0:T(8,128)(2,1)S(1)}, bf16[256,256]{1,0:T(8,128)(2,1)}, u32[]{:S(2)}) copy-start(bf16[256,256]{1,0:T(8,128)(2,1)} %param.21) | copy-start | bytes 393220
  52.1 223.1 %copy-start.5 = (f32[256]{0:T(256)S(1)}, f32[256]{0:T(256)}, u32[]{:S(2)}) copy-start(f32[256]{0:T(256)} %param.22) | copy-start | bytes 3076
  52.1 223.1 %copy-start.7 = (bf16[256]{0:T(256)(128)(2,1)S(1)}, bf16[256]{0:T(256)(128)(2,1)}, u32[]{:S(2)}) copy-start(bf16[256]{0:T(256)(128)(2,1)} %param.23) | copy-start | bytes 1540
  52.1 223.1 %all-to-all-start.1 = ((bf16[256,64,512]{2,1,0:T(8,128)(2,1)}), bf16[256,64,512]{2,1,0:T(8,128)(2,1)}, u32[]{:S(2)}, u32[]{:S(2)}) async-start(bf16[256,64,512]{2,1,0:T(8,128)(2,1)} %broadcast_select_fusion), calls=%async_computation.1 | async-start | bytes 33554432 | tf_op jit(solution)/shard_map/all_to_all | solution.py:122
  285.0 1.3 copy-start.2
  287.0 1.9 copy-start.3
  302.5 1.3 copy-start.2
  304.5 1.9 copy-start.3
  320.0 1.3 copy-start.2
  322.0 1.9 copy-start.3
  337.4 1.3 copy-start.2
  339.4 1.9 copy-start.3
  354.8 1.3 copy-start.2
  356.8 1.9 copy-start.3
  372.2 1.3 copy-start.2
  374.2 1.9 copy-start.3
  389.6 1.3 copy-start.2
  391.6 1.9 copy-start.3
  407.1 1.3 copy-start.2
  409.1 1.9 copy-start.3
  424.5 1.3 copy-start.2
  426.5 1.9 copy-start.3
  441.9 1.3 copy-start.2
  443.9 1.9 copy-start.3
  459.4 1.3 copy-start.2
  461.4 1.9 copy-start.3
  476.8 1.3 copy-start.2
  478.8 1.9 copy-start.3
  484.4 6.1 copy-start.6
  762.0 6.8 copy-start.1
where the time goes:
time: 772 us; the launch traced here: 769 us
  local copies, waits for them, and re-layouts  225 us (29%)
  blocking collectives  220 us (28%)
  waiting for transfers between devices  218 us (28%)
  matrix products  58.9 us (8%)
  other arithmetic  39.8 us (5%)
    all_to_all x1, waiting for transfers between devices, per_device(): lax.all_to_all(served, ('lat', 'lon'), split_axis=0, concat_axis=0, tiled...  218 us
    all_to_all x1, blocking collectives, per_device(): lax.all_to_all(outgoing, ('lat', 'lon'), split_axis=0, concat_axis=0, til...  199 us
    gather x12, local copies, waits for them, and re-layouts, one_group(): jnp.take(arrived, slot_group.reshape(per_group * entries), axis=0)  76.6 us
    scatter x1, local copies, waits for them, and re-layouts, per_device(): outgoing = jnp.zeros((n_slots, n_cells, columns_all), jnp.bfloat16).at[sl...  34.8 us
    reshape x1, local copies, waits for them, and re-layouts, per_device(): returned.reshape(n_slots, n_cells * columns_all)  25 us
    all_to_all x1, blocking collectives, per_device(): lax.all_to_all(wanted, ('lat', 'lon'), split_axis=0, concat_axis=0, tiled...  20.9 us
    dot_general x12, matrix products, decode(): jnp.dot(delta, w_hidden.T, preferred_element_type=jnp.float32)  20.9 us
  transfers between devices with their start and end apart: 1, of which 1 were waited for; matrix products, arithmetic and copies ran while one was open for 0% of the time, Pallas kernels for 0%

commit v1 on v0

v1 whole, which is shorter than its diff:
```python
import jax
import jax.numpy as jnp
from jax import lax
from jax.experimental import pallas as pl
from jax.experimental.pallas import tpu as pltpu
from jax.sharding import PartitionSpec as P

root_coef = 0.7978845608028654
cubic_coef = 0.044715
smooth_sq = 0.01
loss_scale = 64.0

alpha = (1.0 / (root_coef * cubic_coef)) ** (1.0 / 3.0)
beta = root_coef * alpha

AXES = ("lat", "lon")
F32, BF16 = jnp.float32, jnp.bfloat16
VMEM = pl.BlockSpec(memory_space=pltpu.VMEM)
SMEM = pl.BlockSpec(memory_space=pltpu.SMEM)


def three_parts(x):
    high = x.astype(BF16)
    rest = x - high.astype(F32)
    mid = rest.astype(BF16)
    return (high, mid, (rest - mid.astype(F32)).astype(BF16))


def pick(sel, x, dims):
    return sum(
        lax.dot_general(sel, part, (dims, ((), ())), preferred_element_type=F32)
        for part in three_parts(x)
    )


def selectors(owner):
    n = owner.shape[0]
    devices = lax.broadcasted_iota(jnp.int32, (n, 128), 1)
    hit = [(owner[:, e : e + 1] == devices) for e in range(2)]
    both = jnp.where(hit[0] | hit[1], 1.0, 0.0).astype(BF16)
    before = lax.broadcasted_iota(jnp.int32, (n, n), 0) > lax.broadcasted_iota(
        jnp.int32, (n, n), 1
    )
    before = jnp.where(before, 1.0, 0.0).astype(BF16)
    rank = jnp.dot(before, both, preferred_element_type=F32)
    return [
        [jnp.where(hit[e] & (rank == k), 1.0, 0.0) for e in range(2)] for k in range(2)
    ]


def pack_kernel(owner, local, entry, offset, frac, value, weight, out, ids):
    sel = selectors(owner[...])
    off = offset[...]
    row = lax.shift_right_logical(off * 37, 8)
    col = off - row * 7
    pos_lat = frac[:, 0, :] + row.astype(F32)
    pos_lon = frac[:, 1, :] + col.astype(F32)
    data = jnp.concatenate([pos_lat, pos_lon, value[...]], axis=1)
    wts = weight[...]
    where = entry[...]
    wts = jnp.concatenate(
        [jnp.where(where == 0, wts, 0.0), jnp.where(where == 1, wts, 0.0)], axis=0
    )
    loc = local[...].astype(F32) + 1.0
    name = []
    for k in range(2):
        one = (sel[k][0] + sel[k][1]).astype(BF16)
        got = pick(one, data, ((0,), (0,)))
        for f in range(3):
            out[:, k, f, :] = got[:, f * 128 : (f + 1) * 128]
        two = jnp.concatenate(sel[k], axis=0).astype(BF16)
        out[:, k, 3, :] = pick(two, wts, ((0,), (0,)))
        both = jnp.concatenate(
            [jnp.broadcast_to(loc[:, e : e + 1], sel[k][e].shape) for e in range(2)], axis=0
        ).astype(BF16)
        name.append(
            lax.dot_general(two, both, (((0,), (0,)), ((), ())), preferred_element_type=F32)
        )
    lane = lax.broadcasted_iota(jnp.int32, name[0].shape, 1)
    ids[...] = jnp.where(lane == 0, name[0], name[1]).astype(jnp.int32)[:, :2] - 1


def compute_kernel(
    ids,
    latent,
    recv,
    w_hidden,
    b_hidden,
    w_out,
    grad,
    score,
    left,
    deriv,
    total,
    w_t,
    bias,
    head,
    pend,
    pair_p,
    pair_a,
    pair_b,
):
    n_patch = latent.shape[0]
    n_slot = recv.shape[0]
    lane = lax.broadcasted_iota(jnp.int32, (256, 128), 1)

    for p in range(n_patch + 1):
        pend[p] = -1

    def add_slot(s, n):
        p = ids[s]
        at = jnp.where(p < 0, n_patch, p)
        prev = pend[at]
        pair_p[n] = at
        pair_a[n] = prev
        pair_b[n] = s
        full = prev >= 0
        pend[at] = jnp.where(full | (p < 0), -1, s)
        return n + jnp.where(full, 1, 0)

    n_pair = lax.fori_loop(0, n_slot, add_slot, 0)

    def add_rest(p, n):
        prev = pend[p]
        pair_p[n] = p
        pair_a[n] = prev
        pair_b[n] = -1
        return n + jnp.where(prev >= 0, 1, 0)

    n_pair = lax.fori_loop(0, n_patch, add_rest, n_pair)

    w_t[...] = w_hidden[...].astype(F32).T.astype(BF16)
    b_parts = three_parts(jnp.broadcast_to(b_hidden[...] * (1.0 / alpha), (128, 256)).T)
    bias[...] = jnp.where(
        lane == 0,
        b_parts[0],
        jnp.where(lane == 1, b_parts[1], jnp.where(lane == 2, b_parts[2], jnp.zeros_like(b_parts[0]))),
    )
    head[...] = jnp.broadcast_to(w_out[...].astype(F32), (128, 256)).T

    def project(p, c):
        rows = latent[p]
        for m in range(2):
            twice = jnp.concatenate([rows[:, m * 256 : (m + 1) * 256]] * 2, axis=0)
            full = lax.dot_general(
                w_t[...], twice, (((1,), (1,)), ((), ())), preferred_element_type=F32
            ) * (1.0 / alpha)
            high = full.astype(BF16)
            low = (full - high.astype(F32)).astype(BF16)
            left[p, m * 256 : (m + 1) * 256, :] = jnp.where(lane < 64, high, low)
        total[p] = jnp.zeros(total.shape[1:], F32)
        return c

    lax.fori_loop(0, n_patch, project, 0)
    score[...] = jnp.zeros(score.shape, F32)

    cells = lax.broadcasted_iota(jnp.int32, (8, 256), 0).astype(F32)
    ones = jnp.ones((128, 256), BF16)

    def one_pair(i, c):
        p, a, b = pair_p[i], pair_a[i], pair_b[i]
        first, second = recv[a], recv[jnp.maximum(b, 0)]
        obs = jnp.concatenate([first, second], axis=1)
        lat = jnp.maximum(1.0 - jnp.abs(obs[0:1] - cells), 0.0)
        lon = jnp.maximum(1.0 - jnp.abs(obs[1:2] - cells), 0.0)
        corner = jnp.concatenate([lat[r : r + 1] * lon for r in range(8)], axis=0)
        corner_b = corner.astype(BF16)
        right = jnp.concatenate([corner_b, corner_b, ones], axis=0)
        pred = []
        for m in range(2):
            acc = jnp.zeros((8, 256), F32)
            for q in range(4):
                at = m * 256 + q * 64
                lhs = jnp.concatenate(
                    [left[p, at : at + 64, :], bias[q * 64 : q * 64 + 64, :]], axis=1
                )
                v = jnp.dot(lhs, right, preferred_element_type=F32)
                v2 = v * v
                u = jnp.tanh(v * (v2 + beta))
                h = 1.0 + u
                deriv[at : at + 64, :] = (
                    h * (1.0 / 3.0 + (1.0 - u) * (v * (v2 + beta / 3.0)))
                ).astype(BF16)
                wo = head[q * 64 : q * 64 + 64, :]
                act = v * h * jnp.concatenate([wo, wo], axis=1)
                acc = acc + jnp.sum(act.reshape(8, 8, 256), axis=0)
            pred.append(jnp.sum(acc, axis=0, keepdims=True) * (0.5 * alpha))
        value = obs[2:3]
        wts = obs[3:4]
        keep = jnp.where(b >= 0, 1.0, 0.0)
        wts = jnp.concatenate([wts[:, :128], wts[:, 128:] * keep], axis=1)
        e0, e1, between = pred[0] - value, pred[1] - value, pred[0] - pred[1]
        s0, s1, sm = (x * x + smooth_sq for x in (e0, e1, between))
        r0, r1, rm = (lax.rsqrt(x) for x in (s0, s1, sm))
        pen = wts * (0.5 * (s0 * r0 + s1 * r1) - 0.5 * (sm * rm))
        score[pl.ds(a, 1), :] = pen[:, :128]
        score[pl.ds(jnp.where(b < 0, n_slot, b), 1), :] = pen[:, 128:]
        mid = between * rm
        scaled = (0.5 * loss_scale) * wts
        back = jnp.concatenate(
            [corner * (scaled * (e0 * r0 - mid)), corner * (scaled * (e1 * r1 + mid))], axis=0
        ).astype(BF16)
        total[p] += lax.dot_general(
            deriv[...], back, (((1,), (1,)), ((), ())), preferred_element_type=F32
        )
        return c

    lax.fori_loop(0, n_pair, one_pair, 0)

    def finish(p, c):
        both = jnp.where(lane < 64, total[p, 0:256, :], total[p, 256:512, :])
        both = both * (1.5 * head[...])
        high = both.astype(BF16)
        low = (both - high.astype(F32)).astype(BF16)
        dims = (((0,), (0,)), ((), ()))
        res = lax.dot_general(high, w_t[...], dims, preferred_element_type=F32)
        res = res + lax.dot_general(low, w_t[...], dims, preferred_element_type=F32)
        grad[p, :, 0:256] = res[0:64]
        grad[p, :, 256:512] = res[64:128]
        return c

    lax.fori_loop(0, n_patch, finish, 0)


def unpack_kernel(owner, entry, back, out):
    sel = selectors(owner[...])
    got = []
    for e in range(2):
        got.append(
            sum(pick(sel[k][e].astype(BF16), back[:, k, :], ((1,), (0,))) for k in range(2))
        )
    out[...] = jnp.where(entry[...] == 0, got[0], got[1])


def per_device(
    latent,
    patch_owner,
    patch_local,
    obs_patch,
    cell_offset,
    frac,
    obs_value,
    obs_weight,
    w_hidden,
    b_hidden,
    w_out,
):
    n_patch = latent.shape[0]
    limit = pltpu.CompilerParams(vmem_limit_bytes=60 * 1024 * 1024)
    sent, names = pl.pallas_call(
        pack_kernel,
        out_shape=(
            jax.ShapeDtypeStruct((128, 2, 4, 128), F32),
            jax.ShapeDtypeStruct((128, 2), jnp.int32),
        ),
        in_specs=[VMEM] * 7,
        out_specs=(VMEM, VMEM),
        compiler_params=limit,
    )(patch_owner, patch_local, obs_patch, cell_offset, frac, obs_value, obs_weight)
    recv = lax.all_to_all(sent.reshape(256, 4, 128), AXES, 0, 0, tiled=True)
    ids = lax.all_to_all(names, AXES, 0, 0, tiled=True)
    grad, score = pl.pallas_call(
        compute_kernel,
        out_shape=(
            jax.ShapeDtypeStruct(latent.shape, F32),
            jax.ShapeDtypeStruct((264, 128), F32),
        ),
        in_specs=[SMEM] + [VMEM] * 5,
        out_specs=(VMEM, VMEM),
        scratch_shapes=[
            pltpu.VMEM((n_patch, 512, 128), BF16),
            pltpu.VMEM((512, 256), BF16),
            pltpu.VMEM((n_patch, 512, 128), F32),
            pltpu.VMEM((256, 256), BF16),
            pltpu.VMEM((256, 128), BF16),
            pltpu.VMEM((256, 128), F32),
            pltpu.SMEM((n_patch + 1,), jnp.int32),
            pltpu.SMEM((296,), jnp.int32),
            pltpu.SMEM((296,), jnp.int32),
            pltpu.SMEM((296,), jnp.int32),
        ],
        compiler_params=limit,
    )(
        ids.reshape(256),
        latent,
        recv,
        w_hidden,
        b_hidden.reshape(1, 256),
        w_out.reshape(1, 256),
    )
    back = lax.all_to_all(score[:256].reshape(128, 2, 128), AXES, 0, 0, tiled=True)
    obs_score = pl.pallas_call(
        unpack_kernel,
        out_shape=jax.ShapeDtypeStruct(obs_value.shape, F32),
        in_specs=[VMEM] * 3,
        out_specs=VMEM,
        compiler_params=limit,
    )(patch_owner, obs_patch, back)
    return (grad, obs_score)


def solution(mesh):
    rows2 = P(AXES, None)
    rows3 = P(AXES, None, None)
    return jax.shard_map(
        per_device,
        mesh=mesh,
        in_specs=(rows3, rows2, rows2, rows2, rows2, rows3, rows2, rows2, P(), P(), P()),
        out_specs=(rows3, rows2),
        check_vma=False,
    )
```

time: 772 us -> 184 us (0.24)
  local copies, waits for them, and re-layouts: 225 us -> 6.95 us
  waiting for transfers between devices: 218 us -> 10.2 us
  blocking collectives: 220 us -> 38.7 us
  Pallas kernels: 0 us -> 122 us
  matrix products: 58.9 us -> 0 us
  other arithmetic: 39.8 us -> 0.81 us
    all_to_all x1, waiting for transfers between devices: 218 us -> 10.2 us  [per_device(): recv = lax.all_to_all(sent.reshape(256, 4, 128), AXES, 0, 0, tiled=True)]
    all_to_all x2, blocking collectives: 220 us -> 38.7 us  [the longest x1 21.1 us: per_device(): ids = lax.all_to_all(names, AXES, 0, 0, tiled=True)]
    pallas_call x0 -> x3, Pallas kernels: none -> 122 us  [the longest x1 117 us: per_device(): pl.pallas_call(compute_kernel, out_shape=(jax.ShapeDtypeStruct(latent.sha...]
    gather x13 -> x0, local copies, waits for them, and re-layouts: 86.3 us -> none  [the longest x12 76.6 us: one_group(): jnp.take(arrived, slot_group.reshape(per_group * entries), axis=0)]
    dot_general x61 -> x0, matrix products: 58.9 us -> none  [the longest x12 20.9 us: decode(): jnp.dot(delta, w_hidden.T, preferred_element_type=jnp.float32)]
    scatter x2 -> x0, local copies, waits for them, and re-layouts: 36 us -> none  [the longest x1 34.8 us: per_device(): outgoing = jnp.zeros((n_slots, n_cells, columns_all), jnp.bfloat16).at[sl...]
    reshape x38 -> x2, local copies, waits for them, and re-layouts: 36.4 us -> 1.95 us  [the longest x1 1.24 us: per_device(): w_out.reshape(1, 256)]
    select_n x26 -> x0, other arithmetic: 16.8 us -> none  [the longest x1 14.2 us: per_device(): served = jnp.take(latent, jnp.maximum(asked_ids, 0), axis=0)]
  transfers between devices with their start and end apart: 1 -> 1, of which waited for: 1 -> 1; matrix products, arithmetic and copies ran while one was open for 0% -> 2% of each run, Pallas kernels for 0% -> 0%
where the time goes in v1:
time: 184 us; the launch traced here: 183 us
  Pallas kernels  122 us (66%)
  blocking collectives  38.7 us (21%)
  waiting for transfers between devices  10.2 us (6%)
  local copies, waits for them, and re-layouts  6.95 us (4%)
  starting transfers between devices  4.38 us (2%)
    pallas_call x1, Pallas kernels, per_device(): pl.pallas_call(compute_kernel, out_shape=(jax.ShapeDtypeStruct(latent.sha...  117 us
    all_to_all x1, blocking collectives, per_device(): ids = lax.all_to_all(names, AXES, 0, 0, tiled=True)  21.1 us
    all_to_all x1, blocking collectives, per_device(): lax.all_to_all(score[:256].reshape(128, 2, 128), AXES, 0, 0, tiled=True)  17.6 us
    all_to_all x1, waiting for transfers between devices, per_device(): recv = lax.all_to_all(sent.reshape(256, 4, 128), AXES, 0, 0, tiled=True)  10.2 us
    all_to_all x1, starting transfers between devices, per_device(): recv = lax.all_to_all(sent.reshape(256, 4, 128), AXES, 0, 0, tiled=True)  4.38 us
  transfers between devices with their start and end apart: 1, of which 1 were waited for; matrix products, arithmetic and copies ran while one was open for 2% of the time, Pallas kernels for 0%

profile of v1, /device:TPU:1, one launch (start us, length us, event | category | flops | bytes accessed | tf_op | source)
XLA Modules:
  0.0 183.3 jit_solution(10648355643947081837)
XLA Ops:
  0.6 1.4 copy.19.owner
  2.0 1.4 copy.20.local
  3.4 2.7 %shard_map.122 = (f32[128,2,4,128]{3,2,1,0:T(4,128)}, s32[128,2]{1,0:T(8,128)}) custom-call(s32[96,2]{1,0:T(8,128)} %copy.19.owner, s32[96,2]{1,0:T(8,128)} %copy.20.local, s32[96,128]{1,0:T(8,128)} %entry.3, s32[96,128]{1,0:T(8,128)} %offset.1, f32[96,2,128]{2,1,0:T(2,128)} %frac.1, f32[96,128]{1,0:T(8,128)} %value.1, f32[96,128]{1,0:T(8,128)} %weight.1), custom_call_target="tpu_custom_call" | custom-call | tf_op jit(solution)/shard_map/pallas_call | solution.py:250
  6.1 21.1 %all_to_all.19 = s32[128,1,2]{2,1,0:T(1,128)S(1)} all-to-all(s32[128,1,2]{2,1,0:T(1,128)} %bitcast.8), channel_id=1, replica_groups=mesh['lat'=4,'lon'=32] {'lat','lon'}, dimensions={0} | all-to-all | bytes 2048 | tf_op jit(solution)/shard_map/all_to_all | solution.py:261
  27.2 4.4 %all-to-all-start.1 = ((f32[256,4,128]{2,1,0:T(4,128)}), f32[256,4,128]{2,1,0:T(4,128)S(1)}, u32[]{:S(2)}, u32[]{:S(2)}) async-start(f32[256,4,128]{2,1,0:T(4,128)} %bitcast.6), calls=%async_computation.1 | async-start | bytes 1048576 | tf_op jit(solution)/shard_map/all_to_all | solution.py:260
  31.6 1.2 reshape.25.w_out
  32.8 0.5 broadcast.3
  33.3 0.8 reduce.3
  34.2 0.7 reshape.22.ids
  34.9 10.2 %all-to-all-done.1.recv = f32[256,4,128]{2,1,0:T(4,128)S(1)} async-done(((f32[256,4,128]{2,1,0:T(4,128)}), f32[256,4,128]{2,1,0:T(4,128)S(1)}, u32[]{:S(2)}, u32[]{:S(2)}) %all-to-all-start.1) | async-done | bytes 524320 | tf_op jit(solution)/shard_map/all_to_all | solution.py:260
  45.1 0.0 copy-start
  45.1 0.8 copy-done
  45.9 116.5 %shard_map.123 = (f32[32,64,512]{2,1,0:T(8,128)}, f32[264,128]{1,0:T(8,128)}) custom-call(s32[256]{0:T(256)} %reshape.22.ids, bf16[32,64,512]{2,1,0:T(8,128)(2,1)} %latent.1, f32[256,4,128]{2,1,0:T(4,128)} %copy-done, bf16[256,256]{1,0:T(8,128)(2,1)} %w_hidden.1, f32[1,256]{1,0:T(1,128)} %bitcast.9, bf16[1,256]{1,0:T(2,128)(2,1)} %reshape.25.w_out), custom_call_target="tpu_custom_call" | custom-call | tf_op jit(solution)/shard_map/pallas_call | solution.py:262
  162.4 0.9 slice.3
  163.3 17.6 %all_to_all.20.back = f32[128,2,128]{2,1,0:T(2,128)} all-to-all(f32[128,2,128]{2,1,0:T(2,128)S(1)} %bitcast.7), channel_id=1, replica_groups=mesh['lat'=4,'lon'=32] {'lat','lon'}, dimensions={0} | all-to-all | bytes 262144 | tf_op jit(solution)/shard_map/all_to_all | solution.py:291
  180.9 2.4 %shard_map.124 = f32[96,128]{1,0:T(8,128)} custom-call(s32[96,2]{1,0:T(8,128)} %copy.19.owner, s32[96,128]{1,0:T(8,128)} %entry.3, f32[128,2,128]{2,1,0:T(2,128)} %all_to_all.20.back), custom_call_target="tpu_custom_call" | custom-call | tf_op jit(solution)/shard_map/pallas_call | solution.py:292
Async XLA Ops:
  27.2 17.9 %all-to-all-start.1 = ((f32[256,4,128]{2,1,0:T(4,128)}), f32[256,4,128]{2,1,0:T(4,128)S(1)}, u32[]{:S(2)}, u32[]{:S(2)}) async-start(f32[256,4,128]{2,1,0:T(4,128)} %bitcast.6), calls=%async_computation.1 | async-start | bytes 1048576 | tf_op jit(solution)/shard_map/all_to_all | solution.py:260
  45.1 0.8 copy-start

commit v2 on v1

v2 whole, which is shorter than its diff:
```python
import jax
import jax.numpy as jnp
from jax import lax
from jax.experimental import pallas as pl
from jax.experimental.pallas import tpu as pltpu
from jax.sharding import PartitionSpec as P

root_coef = 0.7978845608028654
cubic_coef = 0.044715
smooth_sq = 0.01
loss_scale = 64.0

alpha = (1.0 / (root_coef * cubic_coef)) ** (1.0 / 3.0)
beta = root_coef * alpha

AXES = ("lat", "lon")
F32, BF16 = jnp.float32, jnp.bfloat16
VMEM = pl.BlockSpec(memory_space=pltpu.VMEM)
SMEM = pl.BlockSpec(memory_space=pltpu.SMEM)
UNROLL = 4
TILES = 168


def three_parts(x):
    high = x.astype(BF16)
    rest = x - high.astype(F32)
    mid = rest.astype(BF16)
    return (high, mid, (rest - mid.astype(F32)).astype(BF16))


def pick(sel, x, dims):
    return sum(
        lax.dot_general(sel, part, (dims, ((), ())), preferred_element_type=F32)
        for part in three_parts(x)
    )


def selectors(owner):
    n = owner.shape[0]
    devices = lax.broadcasted_iota(jnp.int32, (n, 128), 1)
    hit = [(owner[:, e : e + 1] == devices) for e in range(2)]
    both = jnp.where(hit[0] | hit[1], 1.0, 0.0).astype(BF16)
    before = lax.broadcasted_iota(jnp.int32, (n, n), 0) > lax.broadcasted_iota(
        jnp.int32, (n, n), 1
    )
    before = jnp.where(before, 1.0, 0.0).astype(BF16)
    rank = jnp.dot(before, both, preferred_element_type=F32)
    return [
        [jnp.where(hit[e] & (rank == k), 1.0, 0.0) for e in range(2)] for k in range(2)
    ]


def ones_before(entry):
    first = lax.broadcasted_iota(jnp.int32, (128, 128), 0)
    second = lax.broadcasted_iota(jnp.int32, (128, 128), 1)
    tri = jnp.where(first < second, 1.0, 0.0).astype(BF16)
    mine = jnp.where(entry == 1, 1.0, 0.0).astype(BF16)
    return jnp.dot(mine, tri, preferred_element_type=F32).astype(jnp.int32)


def pack(owner, local, entry, offset, frac, value, weight, out):
    sel = selectors(owner[...])
    off = offset[...]
    row = lax.shift_right_logical(off * 37, 8)
    col = off - row * 7
    fields = [frac[:, 0, :] + row.astype(F32), frac[:, 1, :] + col.astype(F32)]
    fields += [value[...], weight[...]]
    where = entry[...]
    lane = lax.broadcasted_iota(jnp.int32, where.shape, 1)
    one = ones_before(where)
    loc = local[...].astype(F32) + 1.0
    data, names = [], []
    for e in range(2):
        gap = one if e == 0 else lane - one
        word = jnp.where(where == e, (1 << 20) + gap * 256 + lane, 0)
        for k in range(7):
            come = pltpu.roll(word, 128 - (1 << k), 1)
            stay = jnp.where((word & (256 << k)) == 0, word, 0)
            word = jnp.where((come & (256 << k)) != 0, come, stay)
        source = word & 127
        used = word >= (1 << 20)
        moved = [jnp.take_along_axis(x, source, axis=1) for x in fields]
        moved[3] = jnp.where(used, moved[3], 0.0)
        data.append(jnp.concatenate(moved, axis=1))
        count = jnp.sum(jnp.where(used, 1.0, 0.0), axis=1, keepdims=True)
        names.append(jnp.where(lane < 2, loc[:, e : e + 1], count))
    data = jnp.concatenate(data, axis=0)
    names = jnp.concatenate(names, axis=0).astype(BF16)
    got = []
    for k in range(2):
        two = jnp.concatenate(sel[k], axis=0).astype(BF16)
        rows = pick(two, data, ((0,), (0,)))
        for f in range(4):
            out[:, 4 * k + f, :] = rows[:, f * 128 : (f + 1) * 128]
        got.append(
            lax.dot_general(two, names, (((0,), (0,)), ((), ())), preferred_element_type=F32)
        )
    lane = lax.broadcasted_iota(jnp.int32, (128, 128), 1)
    out[:, 8, :] = jnp.where((lane & 1) == 0, got[0], got[1])


def send_kernel(
    owner,
    local,
    entry,
    offset,
    frac,
    value,
    weight,
    latent,
    w_hidden,
    recv,
    meta,
    left,
    sent,
    w_t,
    send_sem,
    recv_sem,
):
    lat_size, lon_size = lax.axis_size("lat"), lax.axis_size("lon")
    n_dev = lat_size * lon_size
    me = lax.axis_index("lat") * lon_size + lax.axis_index("lon")
    mesh_id = pl.DeviceIdType.MESH

    def place(i):
        j = lax.rem(me + i, n_dev)
        return j, (lax.div(j, lon_size), lax.rem(j, lon_size))

    barrier = pltpu.get_barrier_semaphore()

    def greet(i, c):
        pl.semaphore_signal(barrier, inc=1, device_id=place(i)[1], device_id_type=mesh_id)
        return c

    lax.fori_loop(1, n_dev, greet, 0)
    pack(owner, local, entry, offset, frac, value, weight, sent)
    pl.semaphore_wait(barrier, n_dev - 1)

    def send(i, c):
        j, there = place(i)
        pltpu.make_async_remote_copy(
            src_ref=sent.at[j],
            dst_ref=recv.at[me],
            send_sem=send_sem,
            recv_sem=recv_sem,
            device_id=there,
            device_id_type=mesh_id,
        ).start()
        return c

    lax.fori_loop(1, n_dev, send, 0)
    recv[me] = sent[me]

    w_t[...] = w_hidden[...].astype(F32).T.astype(BF16)
    lane = lax.broadcasted_iota(jnp.int32, (256, 128), 1)

    def project(p, c):
        rows = latent[p]
        for m in range(2):
            twice = jnp.concatenate([rows[:, m * 256 : (m + 1) * 256]] * 2, axis=0)
            full = lax.dot_general(
                w_t[...], twice, (((1,), (1,)), ((), ())), preferred_element_type=F32
            ) * (1.0 / alpha)
            high = full.astype(BF16)
            low = (full - high.astype(F32)).astype(BF16)
            left[p, m * 256 : (m + 1) * 256, :] = jnp.where(lane < 64, high, low)
        return c

    lax.fori_loop(0, latent.shape[0], project, 0)
    pltpu.make_async_remote_copy(
        src_ref=sent.at[pl.ds(0, n_dev - 1)],
        dst_ref=recv.at[pl.ds(0, n_dev - 1)],
        send_sem=send_sem,
        recv_sem=recv_sem,
        device_id=place(1)[1],
        device_id_type=mesh_id,
    ).wait()
    meta[...] = recv[:, 8, :].T[0:8].astype(jnp.int32)


def compute_kernel(
    meta,
    left,
    recv,
    w_hidden,
    b_hidden,
    w_out,
    grad,
    score,
    total,
    w_t,
    bias,
    head,
    comp,
    dense,
    fill,
    tile_p,
    slot_at,
    slot_next,
    *bufs,
):
    n_patch = left.shape[0]
    n_dev = recv.shape[0]
    derivs, pres = bufs[:UNROLL], bufs[UNROLL:]
    lane = lax.broadcasted_iota(jnp.int32, (256, 128), 1)
    lane4 = lax.broadcasted_iota(jnp.int32, (4, 128), 1)
    lane1 = lax.broadcasted_iota(jnp.int32, (1, 128), 1)

    for p in range(n_patch + 1):
        fill[p] = 0
    comp[...] = jnp.zeros(comp.shape, F32)
    dense[...] = jnp.zeros(dense.shape, F32)

    def append(s, n_tile):
        rows = recv[s]
        for k in range(2):
            name, n = meta[k, s], meta[2 + k, s]
            p = jnp.where(name == 0, n_patch, name - 1)
            at = fill[p]
            closed = (at & 255) == 0
            base = jnp.where(closed, n_tile * 256, at)
            tile_p[jnp.where(closed, n_tile, TILES - 1)] = jnp.minimum(p, n_patch - 1)
            n_tile = n_tile + jnp.where(closed & (n > 0), 1, 0)
            half, shift = lax.shift_right_logical(base, 7), base & 127
            odd = half & 1
            over = (odd == 1) & (shift + n > 128)
            after = jnp.where(odd == 1, n_tile * 2, half + 1)
            tile_p[jnp.where(over, n_tile, TILES - 1)] = p
            fill[p] = jnp.where(
                n == 0, at, jnp.where(over, n_tile * 256 + shift + n - 128, base + n)
            )
            n_tile = n_tile + jnp.where(over, 1, 0)
            slot_at[2 * s + k] = base
            slot_next[2 * s + k] = after
            turned = pltpu.roll(rows[4 * k : 4 * k + 4], shift, 1)
            comp[half] = jnp.where(lane4 >= shift, turned, comp[half])
            comp[after] = jnp.where(lane4 < shift, turned, 0.0)
        return n_tile

    n_tile = lax.fori_loop(0, n_dev, append, 0)
    for j in range(UNROLL):
        tile_p[n_tile + j] = 0

    w_t[...] = w_hidden[...].astype(F32).T.astype(BF16)
    b_parts = three_parts(jnp.broadcast_to(b_hidden[...] * (1.0 / alpha), (128, 256)).T)
    column = jnp.where(
        lane == 0,
        b_parts[0],
        jnp.where(
            lane == 1, b_parts[1], jnp.where(lane == 2, b_parts[2], jnp.zeros_like(b_parts[0]))
        ),
    )
    bias[0:256, :] = column
    bias[256:512, :] = column
    head[...] = jnp.broadcast_to(w_out[...].astype(F32), (128, 256)).T

    def clear(p, c):
        total[p] = jnp.zeros(total.shape[1:], F32)
        return c

    lax.fori_loop(0, n_patch, clear, 0)

    cells = lax.broadcasted_iota(jnp.int32, (8, 256), 0).astype(F32)
    ones = jnp.ones((128, 256), BF16)

    def forward(i, deriv, pre):
        obs = jnp.concatenate([comp[2 * i], comp[2 * i + 1]], axis=1)
        lat = jnp.maximum(1.0 - jnp.abs(obs[0:1] - cells), 0.0)
        lon = jnp.maximum(1.0 - jnp.abs(obs[1:2] - cells), 0.0)
        corner = jnp.concatenate([lat[r : r + 1] * lon for r in range(8)], axis=0)
        corner_b = corner.astype(BF16)
        right = jnp.concatenate([corner_b, corner_b, ones], axis=0)
        lhs = jnp.concatenate([left[tile_p[i]], bias[...]], axis=1)
        pre[...] = jnp.dot(lhs, right, preferred_element_type=F32)
        pred = []
        for m in range(2):
            acc = jnp.zeros((8, 256), F32)
            for q in range(4):
                at = m * 256 + q * 64
                v = pre[at : at + 64, :]
                v2 = v * v
                u = jnp.tanh(v * (v2 + beta))
                h = 1.0 + u
                v_b, w_b, h_b = v.astype(BF16), (1.0 - u).astype(BF16), h.astype(BF16)
                slope = v_b * (v_b * v_b + BF16(beta / 3.0))
                deriv[at : at + 64, :] = h_b * (BF16(1.0 / 3.0) + w_b * slope)
                wo = head[q * 64 : q * 64 + 64, :]
                act = v * h * jnp.concatenate([wo, wo], axis=1)
                acc = acc + jnp.sum(act.reshape(8, 8, 256), axis=0)
            pred.append(jnp.sum(acc, axis=0, keepdims=True) * (0.5 * alpha))
        return obs, corner, pred

    def loss(i, obs, pred):
        value = obs[2:3]
        wts = obs[3:4]
        e0, e1, between = pred[0] - value, pred[1] - value, pred[0] - pred[1]
        s0, s1, sm = (x * x + smooth_sq for x in (e0, e1, between))
        r0, r1, rm = (lax.rsqrt(x) for x in (s0, s1, sm))
        pen = wts * (0.5 * (s0 * r0 + s1 * r1) - 0.5 * (sm * rm))
        dense[pl.ds(2 * i, 1), :] = pen[:, :128]
        dense[pl.ds(2 * i + 1, 1), :] = pen[:, 128:]
        mid = between * rm
        scaled = (0.5 * loss_scale) * wts
        return scaled * (e0 * r0 - mid), scaled * (e1 * r1 + mid)

    def backward(i, corner, g, deriv):
        back = jnp.concatenate([corner * g[0], corner * g[1]], axis=0).astype(BF16)
        total[tile_p[i]] += lax.dot_general(
            deriv[...], back, (((1,), (1,)), ((), ())), preferred_element_type=F32
        )

    def some_tiles(i, c):
        base = i * UNROLL
        fw = [forward(base + j, derivs[j], pres[j]) for j in range(UNROLL)]
        gs = [loss(base + j, fw[j][0], fw[j][2]) for j in range(UNROLL)]
        for j in range(UNROLL):
            backward(base + j, fw[j][1], gs[j], derivs[j])
        return c

    lax.fori_loop(0, lax.div(n_tile + UNROLL - 1, UNROLL), some_tiles, 0)

    def give(i, c):
        for j in range(8):
            s = 8 * i + j
            base = slot_at[s]
            half, shift = lax.shift_right_logical(base, 7), base & 127
            row = jnp.where(
                lane1 >= shift, dense[pl.ds(half, 1), :], dense[pl.ds(slot_next[s], 1), :]
            )
            score[pl.ds(s, 1), :] = pltpu.roll(row, (128 - shift) & 127, 1)
        return c

    lax.fori_loop(0, n_dev // 4, give, 0)

    def finish(i, c):
        for j in range(2):
            p = 2 * i + j
            both = jnp.where(lane < 64, total[p, 0:256, :], total[p, 256:512, :])
            both = both * (1.5 * head[...])
            high = both.astype(BF16)
            low = (both - high.astype(F32)).astype(BF16)
            dims = (((0,), (0,)), ((), ()))
            res = lax.dot_general(high, w_t[...], dims, preferred_element_type=F32)
            res = res + lax.dot_general(low, w_t[...], dims, preferred_element_type=F32)
            grad[p, :, 0:256] = res[0:64]
            grad[p, :, 256:512] = res[64:128]
        return c

    lax.fori_loop(0, n_patch // 2, finish, 0)


def unpack_kernel(owner, entry, back, out):
    sel = selectors(owner[...])
    where = entry[...]
    lane = lax.broadcasted_iota(jnp.int32, where.shape, 1)
    one = ones_before(where)
    got = []
    for e in range(2):
        rows = sum(pick(sel[k][e].astype(BF16), back[:, k, :], ((1,), (0,))) for k in range(2))
        got.append(jnp.take_along_axis(rows, one if e == 1 else lane - one, axis=1))
    out[...] = jnp.where(where == 0, got[0], got[1])


def send(patch_owner, patch_local, obs_patch, cell_offset, frac, obs_value, obs_weight, latent, w_hidden):
    n_patch = latent.shape[0]
    return pl.pallas_call(
        send_kernel,
        out_shape=(
            jax.ShapeDtypeStruct((128, 9, 128), F32),
            jax.ShapeDtypeStruct((8, 128), jnp.int32),
            jax.ShapeDtypeStruct((n_patch, 512, 128), BF16),
        ),
        in_specs=[VMEM] * 9,
        out_specs=(VMEM, VMEM, VMEM),
        scratch_shapes=[
            pltpu.VMEM((128, 9, 128), F32),
            pltpu.VMEM((256, 256), BF16),
            pltpu.SemaphoreType.DMA,
            pltpu.SemaphoreType.DMA,
        ],
        compiler_params=pltpu.CompilerParams(
            vmem_limit_bytes=60 * 1024 * 1024, collective_id=0, has_side_effects=True
        ),
    )(patch_owner, patch_local, obs_patch, cell_offset, frac, obs_value, obs_weight, latent, w_hidden)


def compute(meta, left, recv, w_hidden, b_hidden, w_out):
    n_patch = left.shape[0]
    return pl.pallas_call(
        compute_kernel,
        out_shape=(
            jax.ShapeDtypeStruct((n_patch, 64, 512), F32),
            jax.ShapeDtypeStruct((256, 128), F32),
        ),
        in_specs=[SMEM] + [VMEM] * 5,
        out_specs=(VMEM, VMEM),
        scratch_shapes=[
            pltpu.VMEM((n_patch, 512, 128), F32),
            pltpu.VMEM((256, 256), BF16),
            pltpu.VMEM((512, 128), BF16),
            pltpu.VMEM((256, 128), F32),
            pltpu.VMEM((2 * TILES, 4, 128), F32),
            pltpu.VMEM((2 * TILES, 128), F32),
            pltpu.SMEM((n_patch + 1,), jnp.int32),
            pltpu.SMEM((TILES,), jnp.int32),
            pltpu.SMEM((256,), jnp.int32),
            pltpu.SMEM((256,), jnp.int32),
        ]
        + [pltpu.VMEM((512, 256), BF16)] * UNROLL
        + [pltpu.VMEM((512, 256), F32)] * UNROLL,
        compiler_params=pltpu.CompilerParams(vmem_limit_bytes=60 * 1024 * 1024),
    )(meta, left, recv, w_hidden, b_hidden.reshape(1, 256), w_out.reshape(1, 256))


def unpack(patch_owner, obs_patch, back):
    return pl.pallas_call(
        unpack_kernel,
        out_shape=jax.ShapeDtypeStruct(obs_patch.shape, F32),
        in_specs=[VMEM] * 3,
        out_specs=VMEM,
        compiler_params=pltpu.CompilerParams(vmem_limit_bytes=60 * 1024 * 1024),
    )(patch_owner, obs_patch, back)


def per_device(
    latent,
    patch_owner,
    patch_local,
    obs_patch,
    cell_offset,
    frac,
    obs_value,
    obs_weight,
    w_hidden,
    b_hidden,
    w_out,
):
    recv, meta, left = send(
        patch_owner, patch_local, obs_patch, cell_offset, frac, obs_value, obs_weight, latent, w_hidden
    )
    grad, score = compute(meta, left, recv, w_hidden, b_hidden, w_out)
    back = lax.all_to_all(score.reshape(128, 2, 128), AXES, 0, 0, tiled=True)
    return (grad, unpack(patch_owner, obs_patch, back))


def solution(mesh):
    rows2 = P(AXES, None)
    rows3 = P(AXES, None, None)
    return jax.shard_map(
        per_device,
        mesh=mesh,
        in_specs=(rows3, rows2, rows2, rows2, rows2, rows3, rows2, rows2, P(), P(), P()),
        out_specs=(rows3, rows2),
        check_vma=False,
    )
```

time: 184 us -> 100 us (0.54)
  Pallas kernels: 122 us -> 65.7 us
  waiting for transfers between devices: 10.2 us -> 0 us
  blocking collectives: 38.7 us -> 29.7 us
  starting transfers between devices: 4.38 us -> 0 us
  local copies, waits for them, and re-layouts: 6.95 us -> 3.98 us
    pallas_call x3, Pallas kernels: 122 us -> 65.7 us  [the longest x1 39.1 us: compute(): pl.pallas_call(compute_kernel, out_shape=(jax.ShapeDtypeStruct((n_patch,...]
    all_to_all x1 -> x0, waiting for transfers between devices: 10.2 us -> none  [per_device(): recv = lax.all_to_all(sent.reshape(256, 4, 128), AXES, 0, 0, tiled=True)]
    all_to_all x2 -> x1, blocking collectives: 38.7 us -> 29.7 us  [per_device(): back = lax.all_to_all(score.reshape(128, 2, 128), AXES, 0, 0, tiled=True)]
    all_to_all x1 -> x0, starting transfers between devices: 4.38 us -> none  [per_device(): recv = lax.all_to_all(sent.reshape(256, 4, 128), AXES, 0, 0, tiled=True)]
  transfers between devices with their start and end apart: 1 -> 0, of which waited for: 1 -> 0; matrix products, arithmetic and copies ran while one was open for 2% -> 0% of each run, Pallas kernels for 0% -> 0%
where the time goes in v2:
time: 100 us
  Pallas kernels  65.7 us (66%)
  blocking collectives  29.7 us (30%)
  local copies, waits for them, and re-layouts  3.98 us (4%)
    pallas_call x1, Pallas kernels, compute(): pl.pallas_call(compute_kernel, out_shape=(jax.ShapeDtypeStruct((n_patch,...  39.1 us
    all_to_all x1, blocking collectives, per_device(): back = lax.all_to_all(score.reshape(128, 2, 128), AXES, 0, 0, tiled=True)  29.7 us
    pallas_call x1, Pallas kernels, send(): pl.pallas_call(send_kernel, out_shape=(jax.ShapeDtypeStruct((128, 9, 128)...  24.1 us
    unnamed x2, local copies, waits for them, and re-layouts  2.78 us
    pallas_call x1, Pallas kernels, unpack(): pl.pallas_call(unpack_kernel, out_shape=jax.ShapeDtypeStruct(obs_patch.sh...  2.52 us

profile of v2, /device:TPU:1, one launch (start us, length us, event | category | flops | bytes accessed | tf_op | source)
XLA Modules:
  0.0 100.1 jit_solution(10305326861244201927)
XLA Ops:
  0.6 1.2 %reshape.14.w_out = bf16[1,256]{1,0:T(2,128)(2,1)} reshape(bf16[256]{0:T(256)(128)(2,1)} %param.21) | data formatting | bytes 1024 | tf_op jit(solution)/shard_map/reshape | solution.py:412
  1.8 1.4 %copy.13.owner = s32[96,2]{1,0:T(8,128)} copy(s32[96,2]{0,1:T(2,128)} %param.12) | data formatting | bytes 1536 | tf_op args[1]
  3.2 1.4 %copy.14.local = s32[96,2]{1,0:T(8,128)} copy(s32[96,2]{0,1:T(2,128)} %param.13) | data formatting | bytes 1536 | tf_op args[2]
  4.6 24.1 %shard_map.122 = (f32[128,9,128]{2,1,0:T(8,128)}, s32[8,128]{1,0:T(8,128)}, bf16[32,512,128]{2,1,0:T(8,128)(2,1)}) custom-call(s32[96,2]{1,0:T(8,128)} %copy.13.owner, s32[96,2]{1,0:T(8,128)} %copy.14.local, s32[96,128]{1,0:T(8,128)} %entry.3, s32[96,128]{1,0:T(8,128)} %offset.1, f32[96,2,128]{2,1,0:T(2,128)} %frac.1, f32[96,128]{1,0:T(8,128)} %value.1, ...), custom_call_target="tpu_custom_call" | custom-call | tf_op jit(solution)/shard_map/pallas_call | solution.py:366
  28.7 39.1 %shard_map.123 = (f32[32,64,512]{2,1,0:T(8,128)}, f32[256,128]{1,0:T(8,128)}) custom-call(s32[8,128]{1,0:T(8,128)} %get-tuple-element.7.meta, bf16[32,512,128]{2,1,0:T(8,128)(2,1)} %get-tuple-element.8.left, f32[128,9,128]{2,1,0:T(8,128)} %get-tuple-element.9.recv, bf16[256,256]{1,0:T(8,128)(2,1)} %w_hidden.3, f32[1,256]{1,0:T(1,128)} %bitcast.3, ...), custom_call_target="tpu_custom_call" | custom-call | tf_op jit(solution)/shard_map/pallas_call | solution.py:389
  67.8 29.7 %all_to_all.5.back = f32[128,2,128]{2,1,0:T(2,128)} all-to-all(f32[128,2,128]{2,1,0:T(2,128)} %bitcast.2), channel_id=1, replica_groups=mesh['lat'=4,'lon'=32] {'lat','lon'}, dimensions={0} | all-to-all | bytes 262144 | tf_op jit(solution)/shard_map/all_to_all | solution.py:442
  97.6 2.5 %shard_map.124 = f32[96,128]{1,0:T(8,128)} custom-call(s32[96,2]{1,0:T(8,128)} %copy.13.owner, s32[96,128]{1,0:T(8,128)} %entry.3, f32[128,2,128]{2,1,0:T(2,128)} %all_to_all.5.back), custom_call_target="tpu_custom_call" | custom-call | tf_op jit(solution)/shard_map/pallas_call | solution.py:416

commit v3 on v2

--- a/solution.py
+++ b/solution.py
@@ -17,7 +17,8 @@
 F32, BF16 = jnp.float32, jnp.bfloat16
 VMEM = pl.BlockSpec(memory_space=pltpu.VMEM)
 SMEM = pl.BlockSpec(memory_space=pltpu.SMEM)
-UNROLL = 4
+HBM = pl.BlockSpec(memory_space=pl.ANY)
+UNROLL = 2
 TILES = 168
 
 
@@ -33,6 +34,15 @@
         lax.dot_general(sel, part, (dims, ((), ())), preferred_element_type=F32)
         for part in three_parts(x)
     )
+
+
+def columns(rows):
+    n = rows.shape[1]
+    eye = lax.broadcasted_iota(jnp.int32, (n, n), 0) == lax.broadcasted_iota(jnp.int32, (n, n), 1)
+    eye = jnp.where(eye, 1.0, 0.0).astype(BF16)
+    rows = jnp.concatenate([rows.astype(F32)] * 4, axis=0).astype(BF16)
+    dims = (((1,), (1,)), ((), ()))
+    return lax.dot_general(eye, rows, dims, preferred_element_type=F32).astype(jnp.int32)
 
 
 def selectors(owner):
@@ -59,7 +69,7 @@
 
 
 def pack(owner, local, entry, offset, frac, value, weight, out):
-    sel = selectors(owner[...])
+    sel = selectors(columns(owner[...]))
     off = offset[...]
     row = lax.shift_right_logical(off * 37, 8)
     col = off - row * 7
@@ -68,7 +78,7 @@
     where = entry[...]
     lane = lax.broadcasted_iota(jnp.int32, where.shape, 1)
     one = ones_before(where)
-    loc = local[...].astype(F32) + 1.0
+    loc = columns(local[...]).astype(F32) + 1.0
     data, names = [], []
     for e in range(2):
         gap = one if e == 0 else lane - one
@@ -99,6 +109,39 @@
     out[:, 8, :] = jnp.where((lane & 1) == 0, got[0], got[1])
 
 
+def tiling(named, n_patch):
+    flat = named.T
+    name_c = jnp.concatenate([named[:, k : k + 1] for k in range(2)], axis=0)
+    name_r = jnp.concatenate([flat[k : k + 1] for k in range(2)], axis=1)
+    size_r = jnp.concatenate([flat[2 + k : 3 + k] for k in range(2)], axis=1)
+    size_b = jnp.broadcast_to(size_r, (16, 256)).astype(BF16)
+
+    def flag(x):
+        return jnp.where(x, 1.0, 0.0).astype(BF16)
+
+    def iota(shape, axis):
+        return lax.broadcasted_iota(jnp.int32, shape, axis)
+
+    earlier = flag((name_c == name_r) & (iota((256, 256), 0) < iota((256, 256), 1)))
+    inside = jnp.dot(size_b, earlier, preferred_element_type=F32)[0:1]
+    of_patch = flag(name_c == (iota((256, 128), 1) + 1).astype(F32))
+    amount = jnp.dot(size_b, of_patch, preferred_element_type=F32).astype(jnp.int32)
+    tiles = lax.shift_right_logical(amount + 255, 8).astype(F32)
+    below = flag(iota((128, 128), 0) < iota((128, 128), 1))
+    first = jnp.dot(tiles.astype(BF16), below, preferred_element_type=F32)
+    spread = flag((iota((128, 256), 0) + 1).astype(F32) == name_r)
+    start = jnp.dot(first.astype(BF16), spread, preferred_element_type=F32)[0:1]
+    ends = jnp.broadcast_to((first + tiles)[0:1], (128, 128)).T
+    ends = jnp.concatenate([ends, ends], axis=1)
+    owner = jnp.sum(
+        jnp.where(ends <= iota((128, 256), 1).astype(F32), 1.0, 0.0), axis=0, keepdims=True
+    )
+    owner = jnp.minimum(owner, n_patch - 1.0)
+    whole = jnp.broadcast_to(jnp.sum(tiles[0:1], axis=1, keepdims=True), (1, 256))
+    rows = [start * 256.0 + inside, size_r, owner, whole]
+    return jnp.concatenate(rows + rows, axis=0).astype(jnp.int32)
+
+
 def send_kernel(
     owner,
     local,
@@ -107,16 +150,22 @@
     frac,
     value,
     weight,
-    latent,
+    latent_hbm,
     w_hidden,
     recv,
     meta,
+    left_hbm,
+    latent,
     left,
     sent,
     w_t,
     send_sem,
     recv_sem,
+    latent_sem,
+    left_sem,
 ):
+    fetch = pltpu.make_async_copy(latent_hbm, latent, latent_sem)
+    fetch.start()
     lat_size, lon_size = lax.axis_size("lat"), lax.axis_size("lon")
     n_dev = lat_size * lon_size
     me = lax.axis_index("lat") * lon_size + lax.axis_index("lon")
@@ -154,19 +203,37 @@
     w_t[...] = w_hidden[...].astype(F32).T.astype(BF16)
     lane = lax.broadcasted_iota(jnp.int32, (256, 128), 1)
 
-    def project(p, c):
-        rows = latent[p]
-        for m in range(2):
-            twice = jnp.concatenate([rows[:, m * 256 : (m + 1) * 256]] * 2, axis=0)
-            full = lax.dot_general(
-                w_t[...], twice, (((1,), (1,)), ((), ())), preferred_element_type=F32
-            ) * (1.0 / alpha)
-            high = full.astype(BF16)
-            low = (full - high.astype(F32)).astype(BF16)
-            left[p, m * 256 : (m + 1) * 256, :] = jnp.where(lane < 64, high, low)
-        return c
-
-    lax.fori_loop(0, latent.shape[0], project, 0)
+    def leave(p, j):
+        return pltpu.make_async_copy(left.at[j], left_hbm.at[p], left_sem.at[j])
+
+    fetch.wait()
+
+    def project(i, c):
+        for j in range(2):
+            p = 2 * i + j
+
+            @pl.when(i > 0)
+            def _():
+                leave(p - 2, j).wait()
+
+            for m in range(2):
+                rows = latent[p, :, m * 256 : (m + 1) * 256]
+                full = lax.dot_general(
+                    w_t[...],
+                    jnp.concatenate([rows, rows], axis=0),
+                    (((1,), (1,)), ((), ())),
+                    preferred_element_type=F32,
+                ) * (1.0 / alpha)
+                high = full.astype(BF16)
+                low = (full - high.astype(F32)).astype(BF16)
+                left[j, m * 256 : (m + 1) * 256, :] = jnp.where(lane < 64, high, low)
+            leave(p, j).start()
+        return c
+
+    n_patch = latent.shape[0]
+    lax.fori_loop(0, n_patch // 2, project, 0)
+    for j in range(2):
+        leave(n_patch - 2 + j, j).wait()
     pltpu.make_async_remote_copy(
         src_ref=sent.at[pl.ds(0, n_dev - 1)],
         dst_ref=recv.at[pl.ds(0, n_dev - 1)],
@@ -175,71 +242,61 @@
         device_id=place(1)[1],
         device_id_type=mesh_id,
     ).wait()
-    meta[...] = recv[:, 8, :].T[0:8].astype(jnp.int32)
+    meta[...] = tiling(recv[:, 8, :], latent.shape[0])
 
 
 def compute_kernel(
     meta,
-    left,
+    left_hbm,
     recv,
     w_hidden,
     b_hidden,
     w_out,
     grad,
     score,
+    left,
     total,
     w_t,
     bias,
     head,
     comp,
     dense,
-    fill,
-    tile_p,
-    slot_at,
-    slot_next,
+    ready,
+    left_sem,
+    grad_sem,
     *bufs,
 ):
     n_patch = left.shape[0]
     n_dev = recv.shape[0]
-    derivs, pres = bufs[:UNROLL], bufs[UNROLL:]
+    derivs, pres, spreads, backs = (bufs[i * UNROLL : (i + 1) * UNROLL] for i in range(4))
     lane = lax.broadcasted_iota(jnp.int32, (256, 128), 1)
     lane4 = lax.broadcasted_iota(jnp.int32, (4, 128), 1)
     lane1 = lax.broadcasted_iota(jnp.int32, (1, 128), 1)
 
-    for p in range(n_patch + 1):
-        fill[p] = 0
+    fetch = pltpu.make_async_copy(left_hbm, left, left_sem)
+    fetch.start()
+    n_tile = meta[3, 0]
+
+    def tile_of(i):
+        return meta[2, i]
+
     comp[...] = jnp.zeros(comp.shape, F32)
     dense[...] = jnp.zeros(dense.shape, F32)
 
-    def append(s, n_tile):
-        rows = recv[s]
-        for k in range(2):
-            name, n = meta[k, s], meta[2 + k, s]
-            p = jnp.where(name == 0, n_patch, name - 1)
-            at = fill[p]
-            closed = (at & 255) == 0
-            base = jnp.where(closed, n_tile * 256, at)
-            tile_p[jnp.where(closed, n_tile, TILES - 1)] = jnp.minimum(p, n_patch - 1)
-            n_tile = n_tile + jnp.where(closed & (n > 0), 1, 0)
-            half, shift = lax.shift_right_logical(base, 7), base & 127
-            odd = half & 1
-            over = (odd == 1) & (shift + n > 128)
-            after = jnp.where(odd == 1, n_tile * 2, half + 1)
-            tile_p[jnp.where(over, n_tile, TILES - 1)] = p
-            fill[p] = jnp.where(
-                n == 0, at, jnp.where(over, n_tile * 256 + shift + n - 128, base + n)
-            )
-            n_tile = n_tile + jnp.where(over, 1, 0)
-            slot_at[2 * s + k] = base
-            slot_next[2 * s + k] = after
-            turned = pltpu.roll(rows[4 * k : 4 * k + 4], shift, 1)
-            comp[half] = jnp.where(lane4 >= shift, turned, comp[half])
-            comp[after] = jnp.where(lane4 < shift, turned, 0.0)
-        return n_tile
-
-    n_tile = lax.fori_loop(0, n_dev, append, 0)
-    for j in range(UNROLL):
-        tile_p[n_tile + j] = 0
+    def append(i, c):
+        for j in range(8):
+            s = 8 * i + j
+            rows = recv[s, 0:8, :]
+            for k in range(2):
+                base, n = meta[0, 128 * k + s], meta[1, 128 * k + s]
+                half, shift = lax.shift_right_logical(base, 7), base & 127
+                turned = pltpu.roll(rows[4 * k : 4 * k + 4], shift, 1)
+                end = shift + n
+                pltpu.store(comp.at[half], turned, mask=(lane4 >= shift) & (lane4 < end))
+                pltpu.store(comp.at[half + 1], turned, mask=lane4 < end - 128)
+        return c
+
+    lax.fori_loop(0, n_dev // 8, append, 0)
 
     w_t[...] = w_hidden[...].astype(F32).T.astype(BF16)
     b_parts = three_parts(jnp.broadcast_to(b_hidden[...] * (1.0 / alpha), (128, 256)).T)
@@ -252,26 +309,30 @@
     )
     bias[0:256, :] = column
     bias[256:512, :] = column
-    head[...] = jnp.broadcast_to(w_out[...].astype(F32), (128, 256)).T
+    head[...] = jnp.broadcast_to(w_out[...].astype(F32).reshape(1, 256), (128, 256)).T
 
     def clear(p, c):
         total[p] = jnp.zeros(total.shape[1:], F32)
         return c
 
     lax.fori_loop(0, n_patch, clear, 0)
+    fetch.wait()
 
     cells = lax.broadcasted_iota(jnp.int32, (8, 256), 0).astype(F32)
     ones = jnp.ones((128, 256), BF16)
 
-    def forward(i, deriv, pre):
+    def hidden(i, pre, spread):
         obs = jnp.concatenate([comp[2 * i], comp[2 * i + 1]], axis=1)
         lat = jnp.maximum(1.0 - jnp.abs(obs[0:1] - cells), 0.0)
         lon = jnp.maximum(1.0 - jnp.abs(obs[1:2] - cells), 0.0)
         corner = jnp.concatenate([lat[r : r + 1] * lon for r in range(8)], axis=0)
+        spread[...] = corner
         corner_b = corner.astype(BF16)
         right = jnp.concatenate([corner_b, corner_b, ones], axis=0)
-        lhs = jnp.concatenate([left[tile_p[i]], bias[...]], axis=1)
+        lhs = jnp.concatenate([left[tile_of(i)], bias[...]], axis=1)
         pre[...] = jnp.dot(lhs, right, preferred_element_type=F32)
+
+    def gelu(i, pre, deriv):
         pred = []
         for m in range(2):
             acc = jnp.zeros((8, 256), F32)
@@ -288,69 +349,97 @@
                 act = v * h * jnp.concatenate([wo, wo], axis=1)
                 acc = acc + jnp.sum(act.reshape(8, 8, 256), axis=0)
             pred.append(jnp.sum(acc, axis=0, keepdims=True) * (0.5 * alpha))
-        return obs, corner, pred
-
-    def loss(i, obs, pred):
+        return pred
+
+    def loss(i, pred):
+        obs = jnp.concatenate([comp[2 * i], comp[2 * i + 1]], axis=1)
         value = obs[2:3]
         wts = obs[3:4]
         e0, e1, between = pred[0] - value, pred[1] - value, pred[0] - pred[1]
         s0, s1, sm = (x * x + smooth_sq for x in (e0, e1, between))
         r0, r1, rm = (lax.rsqrt(x) for x in (s0, s1, sm))
         pen = wts * (0.5 * (s0 * r0 + s1 * r1) - 0.5 * (sm * rm))
-        dense[pl.ds(2 * i, 1), :] = pen[:, :128]
-        dense[pl.ds(2 * i + 1, 1), :] = pen[:, 128:]
         mid = between * rm
         scaled = (0.5 * loss_scale) * wts
-        return scaled * (e0 * r0 - mid), scaled * (e1 * r1 + mid)
-
-    def backward(i, corner, g, deriv):
-        back = jnp.concatenate([corner * g[0], corner * g[1]], axis=0).astype(BF16)
-        total[tile_p[i]] += lax.dot_general(
-            deriv[...], back, (((1,), (1,)), ((), ())), preferred_element_type=F32
+        return scaled * (e0 * r0 - mid), scaled * (e1 * r1 + mid), pen
+
+    def keep(i, pen):
+        dense[pl.ds(2 * i + 2, 1), :] = pen[:, :128]
+        dense[pl.ds(2 * i + 3, 1), :] = pen[:, 128:]
+
+    def make_back(spread, g, back):
+        corner = spread[...]
+        back[...] = jnp.concatenate([corner * g[0], corner * g[1]], axis=0).astype(BF16)
+
+    def backward(i, back, deriv):
+        both = lax.dot_general(
+            deriv[...], back[...], (((1,), (1,)), ((), ())), preferred_element_type=F32
         )
-
-    def some_tiles(i, c):
+        total[tile_of(jnp.maximum(i, 0))] += jnp.where(lane < 64, both[0:256], both[256:512])
+
+    def some_tiles(i, pen):
         base = i * UNROLL
-        fw = [forward(base + j, derivs[j], pres[j]) for j in range(UNROLL)]
-        gs = [loss(base + j, fw[j][0], fw[j][2]) for j in range(UNROLL)]
         for j in range(UNROLL):
-            backward(base + j, fw[j][1], gs[j], derivs[j])
-        return c
-
-    lax.fori_loop(0, lax.div(n_tile + UNROLL - 1, UNROLL), some_tiles, 0)
+            after, prev = (j + 1) % UNROLL, (j + UNROLL - 1) % UNROLL
+            hidden(base + j + 1, pres[after], spreads[after])
+            pred = gelu(base + j, pres[j], derivs[j])
+            keep(base + j - 1, pen)
+            backward(base + j - 1, backs[prev], derivs[prev])
+            g0, g1, pen = loss(base + j, pred)
+            make_back(spreads[j], (g0, g1), backs[j])
+        return pen
+
+    hidden(0, pres[0], spreads[0])
+    backs[UNROLL - 1][...] = jnp.zeros((128, 256), BF16)
+    derivs[UNROLL - 1][...] = jnp.zeros((512, 256), BF16)
+    steps = lax.div(n_tile + UNROLL - 1, UNROLL)
+    pen = lax.fori_loop(0, steps, some_tiles, jnp.zeros((1, 256), F32))
+    keep(steps * UNROLL - 1, pen)
+    backward(steps * UNROLL - 1, backs[UNROLL - 1], derivs[UNROLL - 1])
 
     def give(i, c):
         for j in range(8):
             s = 8 * i + j
-            base = slot_at[s]
-            half, shift = lax.shift_right_logical(base, 7), base & 127
-            row = jnp.where(
-                lane1 >= shift, dense[pl.ds(half, 1), :], dense[pl.ds(slot_next[s], 1), :]
-            )
-            score[pl.ds(s, 1), :] = pltpu.roll(row, (128 - shift) & 127, 1)
-        return c
-
-    lax.fori_loop(0, n_dev // 4, give, 0)
+            for k in range(2):
+                base = meta[0, 128 * k + s]
+                half, shift = lax.shift_right_logical(base, 7), base & 127
+                row = jnp.where(
+                    lane1 >= shift, dense[pl.ds(half + 2, 1), :], dense[pl.ds(half + 3, 1), :]
+                )
+                score[pl.ds(2 * s + k, 1), :] = pltpu.roll(row, (128 - shift) & 127, 1)
+        return c
+
+    lax.fori_loop(0, n_dev // 8, give, 0)
+
+    def leave(p, j):
+        return pltpu.make_async_copy(ready.at[j], grad.at[p], grad_sem.at[j])
 
     def finish(i, c):
         for j in range(2):
             p = 2 * i + j
-            both = jnp.where(lane < 64, total[p, 0:256, :], total[p, 256:512, :])
-            both = both * (1.5 * head[...])
+            both = total[p] * (1.5 * head[...])
             high = both.astype(BF16)
             low = (both - high.astype(F32)).astype(BF16)
             dims = (((0,), (0,)), ((), ()))
             res = lax.dot_general(high, w_t[...], dims, preferred_element_type=F32)
             res = res + lax.dot_general(low, w_t[...], dims, preferred_element_type=F32)
-            grad[p, :, 0:256] = res[0:64]
-            grad[p, :, 256:512] = res[64:128]
+
+            @pl.when(i > 0)
+            def _():
+                leave(p - 2, j).wait()
+
+            ready[j, :, 0:256] = res[0:64]
+            ready[j, :, 256:512] = res[64:128]
+            leave(p, j).start()
         return c
 
     lax.fori_loop(0, n_patch // 2, finish, 0)
+    for j in range(2):
+        leave(n_patch - 2 + j, j).wait()
 
 
 def unpack_kernel(owner, entry, back, out):
-    sel = selectors(owner[...])
+    sel = selectors(columns(owner[...]))
     where = entry[...]
     lane = lax.broadcasted_iota(jnp.int32, where.shape, 1)
     one = ones_before(where)
@@ -367,16 +456,20 @@
         send_kernel,
         out_shape=(
             jax.ShapeDtypeStruct((128, 9, 128), F32),
-            jax.ShapeDtypeStruct((8, 128), jnp.int32),
+            jax.ShapeDtypeStruct((8, 256), jnp.int32),
             jax.ShapeDtypeStruct((n_patch, 512, 128), BF16),
         ),
-        in_specs=[VMEM] * 9,
-        out_specs=(VMEM, VMEM, VMEM),
+        in_specs=[VMEM] * 7 + [HBM, VMEM],
+        out_specs=(VMEM, VMEM, HBM),
         scratch_shapes=[
+            pltpu.VMEM(latent.shape, BF16),
+            pltpu.VMEM((2, 512, 128), BF16),
             pltpu.VMEM((128, 9, 128), F32),
             pltpu.VMEM((256, 256), BF16),
             pltpu.SemaphoreType.DMA,
             pltpu.SemaphoreType.DMA,
+            pltpu.SemaphoreType.DMA,
+            pltpu.SemaphoreType.DMA((2,)),
         ],
         compiler_params=pltpu.CompilerParams(
             vmem_limit_bytes=60 * 1024 * 1024, collective_id=0, has_side_effects=True
@@ -392,24 +485,26 @@
             jax.ShapeDtypeStruct((n_patch, 64, 512), F32),
             jax.ShapeDtypeStruct((256, 128), F32),
         ),
-        in_specs=[SMEM] + [VMEM] * 5,
-        out_specs=(VMEM, VMEM),
+        in_specs=[SMEM, HBM] + [VMEM] * 4,
+        out_specs=(HBM, VMEM),
         scratch_shapes=[
-            pltpu.VMEM((n_patch, 512, 128), F32),
+            pltpu.VMEM(left.shape, BF16),
+            pltpu.VMEM((n_patch, 256, 128), F32),
             pltpu.VMEM((256, 256), BF16),
             pltpu.VMEM((512, 128), BF16),
             pltpu.VMEM((256, 128), F32),
             pltpu.VMEM((2 * TILES, 4, 128), F32),
-            pltpu.VMEM((2 * TILES, 128), F32),
-            pltpu.SMEM((n_patch + 1,), jnp.int32),
-            pltpu.SMEM((TILES,), jnp.int32),
-            pltpu.SMEM((256,), jnp.int32),
-            pltpu.SMEM((256,), jnp.int32),
+            pltpu.VMEM((2 * TILES + 8, 128), F32),
+            pltpu.VMEM((2, 64, 512), F32),
+            pltpu.SemaphoreType.DMA,
+            pltpu.SemaphoreType.DMA((2,)),
         ]
         + [pltpu.VMEM((512, 256), BF16)] * UNROLL
-        + [pltpu.VMEM((512, 256), F32)] * UNROLL,
+        + [pltpu.VMEM((512, 256), F32)] * UNROLL
+        + [pltpu.VMEM((64, 256), F32)] * UNROLL
+        + [pltpu.VMEM((128, 256), BF16)] * UNROLL,
         compiler_params=pltpu.CompilerParams(vmem_limit_bytes=60 * 1024 * 1024),
-    )(meta, left, recv, w_hidden, b_hidden.reshape(1, 256), w_out.reshape(1, 256))
+    )(meta, left, recv, w_hidden, b_hidden.reshape(1, 256), w_out)
 
 
 def unpack(patch_owner, obs_patch, back):
@@ -436,11 +531,11 @@
     w_out,
 ):
     recv, meta, left = send(
-        patch_owner, patch_local, obs_patch, cell_offset, frac, obs_value, obs_weight, latent, w_hidden
+        patch_owner.T, patch_local.T, obs_patch, cell_offset, frac, obs_value, obs_weight, latent, w_hidden
     )
     grad, score = compute(meta, left, recv, w_hidden, b_hidden, w_out)
     back = lax.all_to_all(score.reshape(128, 2, 128), AXES, 0, 0, tiled=True)
-    return (grad, unpack(patch_owner, obs_patch, back))
+    return (grad, unpack(patch_owner.T, obs_patch, back))
 
 
 def solution(mesh):

time: 100 us -> 92.7 us (0.927)
  blocking collectives: 29.7 us -> 15.9 us
  Pallas kernels: 65.7 us -> 75.9 us
  local copies, waits for them, and re-layouts: 3.98 us -> 0 us
    all_to_all x1, blocking collectives: 29.7 us -> 15.9 us  [per_device(): back = lax.all_to_all(score.reshape(128, 2, 128), AXES, 0, 0, tiled=True)]
    pallas_call x1, Pallas kernels: 39.1 us -> 44.6 us  [compute(): pl.pallas_call(compute_kernel, out_shape=(jax.ShapeDtypeStruct((n_patch,...]
    pallas_call x1, Pallas kernels: 24.1 us -> 28.7 us  [send(): pl.pallas_call(send_kernel, out_shape=(jax.ShapeDtypeStruct((128, 9, 128)...]
    unnamed x2 -> x0, local copies, waits for them, and re-layouts: 2.78 us -> none
    reshape x1 -> x0, local copies, waits for them, and re-layouts: 1.2 us -> none  [compute(): w_out.reshape(1, 256)]
where the time goes in v3:
time: 92.7 us; the launch traced here: 92.4 us
  Pallas kernels  75.9 us (82%)
  blocking collectives  15.9 us (17%)
    pallas_call x1, Pallas kernels, compute(): pl.pallas_call(compute_kernel, out_shape=(jax.ShapeDtypeStruct((n_patch,...  44.6 us
    pallas_call x1, Pallas kernels, send(): pl.pallas_call(send_kernel, out_shape=(jax.ShapeDtypeStruct((128, 9, 128)...  28.7 us
    all_to_all x1, blocking collectives, per_device(): back = lax.all_to_all(score.reshape(128, 2, 128), AXES, 0, 0, tiled=True)  15.9 us
    pallas_call x1, Pallas kernels, unpack(): pl.pallas_call(unpack_kernel, out_shape=jax.ShapeDtypeStruct(obs_patch.sh...  2.63 us

profile of v3, /device:TPU:1, one launch (start us, length us, event | category | flops | bytes accessed | tf_op | source)
XLA Modules:
  0.0 92.4 jit_solution(7537535453581971336)
XLA Ops:
  0.6 28.7 %shard_map.122 = (f32[128,9,128]{2,1,0:T(8,128)}, s32[8,256]{1,0:T(8,128)}, bf16[32,512,128]{2,1,0:T(8,128)(2,1)}) custom-call(s32[2,96]{1,0:T(2,128)} %bitcast.5, s32[2,96]{1,0:T(2,128)} %bitcast.7, s32[96,128]{1,0:T(8,128)} %entry.3, s32[96,128]{1,0:T(8,128)} %offset.1, f32[96,2,128]{2,1,0:T(2,128)} %frac.1, f32[96,128]{1,0:T(8,128)} %value.1, ...), custom_call_target="tpu_custom_call" | custom-call | tf_op jit(solution)/shard_map/pallas_call | solution.py:455
  29.3 44.6 %shard_map.123 = (f32[32,64,512]{2,1,0:T(8,128)}, f32[256,128]{1,0:T(8,128)}) custom-call(s32[8,256]{1,0:T(8,128)} %get-tuple-element.7.meta, bf16[32,512,128]{2,1,0:T(8,128)(2,1)} %get-tuple-element.8.left_hbm, f32[128,9,128]{2,1,0:T(8,128)} %get-tuple-element.9.recv, bf16[256,256]{1,0:T(8,128)(2,1)} %w_hidden.3, f32[1,256]{1,0:T(1,128)} %bitcast.8, ...), custom_call_target="tpu_custom_call" | custom-call | tf_op jit(solution)/shard_map/pallas_call | solution.py:482
  73.9 15.9 %all_to_all.5.back = f32[128,2,128]{2,1,0:T(2,128)} all-to-all(f32[128,2,128]{2,1,0:T(2,128)} %bitcast.4), channel_id=1, replica_groups=mesh['lat'=4,'lon'=32] {'lat','lon'}, dimensions={0} | all-to-all | bytes 262144 | tf_op jit(solution)/shard_map/all_to_all | solution.py:537
  89.8 2.6 %shard_map.124 = f32[96,128]{1,0:T(8,128)} custom-call(s32[2,96]{1,0:T(2,128)} %bitcast.6, s32[96,128]{1,0:T(8,128)} %entry.3, f32[128,2,128]{2,1,0:T(2,128)} %all_to_all.5.back), custom_call_target="tpu_custom_call" | custom-call | tf_op jit(solution)/shard_map/pallas_call | solution.py:511

commit v4 on v3

--- a/solution.py
+++ b/solution.py
@@ -203,19 +203,14 @@
     w_t[...] = w_hidden[...].astype(F32).T.astype(BF16)
     lane = lax.broadcasted_iota(jnp.int32, (256, 128), 1)
 
-    def leave(p, j):
-        return pltpu.make_async_copy(left.at[j], left_hbm.at[p], left_sem.at[j])
+    def leave(p):
+        return pltpu.make_async_copy(left.at[p], left_hbm.at[p], left_sem)
 
     fetch.wait()
 
     def project(i, c):
-        for j in range(2):
-            p = 2 * i + j
-
-            @pl.when(i > 0)
-            def _():
-                leave(p - 2, j).wait()
-
+        for j in range(4):
+            p = 4 * i + j
             for m in range(2):
                 rows = latent[p, :, m * 256 : (m + 1) * 256]
                 full = lax.dot_general(
@@ -226,14 +221,12 @@
                 ) * (1.0 / alpha)
                 high = full.astype(BF16)
                 low = (full - high.astype(F32)).astype(BF16)
-                left[j, m * 256 : (m + 1) * 256, :] = jnp.where(lane < 64, high, low)
-            leave(p, j).start()
+                left[p, m * 256 : (m + 1) * 256, :] = jnp.where(lane < 64, high, low)
+            leave(p).start()
         return c
 
     n_patch = latent.shape[0]
-    lax.fori_loop(0, n_patch // 2, project, 0)
-    for j in range(2):
-        leave(n_patch - 2 + j, j).wait()
+    lax.fori_loop(0, n_patch // 4, project, 0)
     pltpu.make_async_remote_copy(
         src_ref=sent.at[pl.ds(0, n_dev - 1)],
         dst_ref=recv.at[pl.ds(0, n_dev - 1)],
@@ -242,7 +235,8 @@
         device_id=place(1)[1],
         device_id_type=mesh_id,
     ).wait()
-    meta[...] = tiling(recv[:, 8, :], latent.shape[0])
+    meta[...] = tiling(recv[:, 8, :], n_patch)
+    pltpu.make_async_copy(left, left_hbm, left_sem).wait()
 
 
 def compute_kernel(
@@ -411,12 +405,12 @@
 
     lax.fori_loop(0, n_dev // 8, give, 0)
 
-    def leave(p, j):
-        return pltpu.make_async_copy(ready.at[j], grad.at[p], grad_sem.at[j])
+    def leave(p):
+        return pltpu.make_async_copy(ready.at[p], grad.at[p], grad_sem)
 
     def finish(i, c):
-        for j in range(2):
-            p = 2 * i + j
+        for j in range(4):
+            p = 4 * i + j
             both = total[p] * (1.5 * head[...])
             high = both.astype(BF16)
             low = (both - high.astype(F32)).astype(BF16)
@@ -424,18 +418,13 @@
             res = lax.dot_general(high, w_t[...], dims, preferred_element_type=F32)
             res = res + lax.dot_general(low, w_t[...], dims, preferred_element_type=F32)
 
-            @pl.when(i > 0)
-            def _():
-                leave(p - 2, j).wait()
-
-            ready[j, :, 0:256] = res[0:64]
-            ready[j, :, 256:512] = res[64:128]
-            leave(p, j).start()
-        return c
-
-    lax.fori_loop(0, n_patch // 2, finish, 0)
-    for j in range(2):
-        leave(n_patch - 2 + j, j).wait()
+            ready[p, :, 0:256] = res[0:64]
+            ready[p, :, 256:512] = res[64:128]
+            leave(p).start()
+        return c
+
+    lax.fori_loop(0, n_patch // 4, finish, 0)
+    pltpu.make_async_copy(ready, grad, grad_sem).wait()
 
 
 def unpack_kernel(owner, entry, back, out):
@@ -463,13 +452,13 @@
         out_specs=(VMEM, VMEM, HBM),
         scratch_shapes=[
             pltpu.VMEM(latent.shape, BF16),
-            pltpu.VMEM((2, 512, 128), BF16),
+            pltpu.VMEM((latent.shape[0], 512, 128), BF16),
             pltpu.VMEM((128, 9, 128), F32),
             pltpu.VMEM((256, 256), BF16),
             pltpu.SemaphoreType.DMA,
             pltpu.SemaphoreType.DMA,
             pltpu.SemaphoreType.DMA,
-            pltpu.SemaphoreType.DMA((2,)),
+            pltpu.SemaphoreType.DMA,
         ],
         compiler_params=pltpu.CompilerParams(
             vmem_limit_bytes=60 * 1024 * 1024, collective_id=0, has_side_effects=True
@@ -495,9 +484,9 @@
             pltpu.VMEM((256, 128), F32),
             pltpu.VMEM((2 * TILES, 4, 128), F32),
             pltpu.VMEM((2 * TILES + 8, 128), F32),
-            pltpu.VMEM((2, 64, 512), F32),
+            pltpu.VMEM((n_patch, 64, 512), F32),
             pltpu.SemaphoreType.DMA,
-            pltpu.SemaphoreType.DMA((2,)),
+            pltpu.SemaphoreType.DMA,
         ]
         + [pltpu.VMEM((512, 256), BF16)] * UNROLL
         + [pltpu.VMEM((512, 256), F32)] * UNROLL

time: 92.7 us -> 82.3 us (0.89)
  Pallas kernels: 75.9 us -> 52.2 us
  blocking collectives: 15.9 us -> 29.3 us
    pallas_call x1, Pallas kernels: 44.6 us -> 26.7 us  [compute(): pl.pallas_call(compute_kernel, out_shape=(jax.ShapeDtypeStruct((n_patch,...]
    all_to_all x1, blocking collectives: 15.9 us -> 29.3 us  [per_device(): back = lax.all_to_all(score.reshape(128, 2, 128), AXES, 0, 0, tiled=True)]
    pallas_call x1, Pallas kernels: 28.7 us -> 22.9 us  [send(): pl.pallas_call(send_kernel, out_shape=(jax.ShapeDtypeStruct((128, 9, 128)...]
where the time goes in v4:
time: 82.3 us; the launch traced here: 82.1 us
  Pallas kernels  52.2 us (63%)
  blocking collectives  29.3 us (36%)
    all_to_all x1, blocking collectives, per_device(): back = lax.all_to_all(score.reshape(128, 2, 128), AXES, 0, 0, tiled=True)  29.3 us
    pallas_call x1, Pallas kernels, compute(): pl.pallas_call(compute_kernel, out_shape=(jax.ShapeDtypeStruct((n_patch,...  26.7 us
    pallas_call x1, Pallas kernels, send(): pl.pallas_call(send_kernel, out_shape=(jax.ShapeDtypeStruct((128, 9, 128)...  22.9 us
    pallas_call x1, Pallas kernels, unpack(): pl.pallas_call(unpack_kernel, out_shape=jax.ShapeDtypeStruct(obs_patch.sh...  2.63 us

profile of v4, /device:TPU:1, one launch (start us, length us, event | category | flops | bytes accessed | tf_op | source)
XLA Modules:
  0.0 82.1 jit_solution(16509401738764091070)
XLA Ops:
  0.6 22.9 %shard_map.122 = (f32[128,9,128]{2,1,0:T(8,128)}, s32[8,256]{1,0:T(8,128)}, bf16[32,512,128]{2,1,0:T(8,128)(2,1)}) custom-call(s32[2,96]{1,0:T(2,128)} %bitcast.5, s32[2,96]{1,0:T(2,128)} %bitcast.7, s32[96,128]{1,0:T(8,128)} %entry.3, s32[96,128]{1,0:T(8,128)} %offset.1, f32[96,2,128]{2,1,0:T(2,128)} %frac.1, f32[96,128]{1,0:T(8,128)} %value.1, ...), custom_call_target="tpu_custom_call" | custom-call | tf_op jit(solution)/shard_map/pallas_call | solution.py:444
  23.5 26.7 %shard_map.123 = (f32[32,64,512]{2,1,0:T(8,128)}, f32[256,128]{1,0:T(8,128)}) custom-call(s32[8,256]{1,0:T(8,128)} %get-tuple-element.7.meta, bf16[32,512,128]{2,1,0:T(8,128)(2,1)} %get-tuple-element.8.left_hbm, f32[128,9,128]{2,1,0:T(8,128)} %get-tuple-element.9.recv, bf16[256,256]{1,0:T(8,128)(2,1)} %w_hidden.3, f32[1,256]{1,0:T(1,128)} %bitcast.8, ...), custom_call_target="tpu_custom_call" | custom-call | tf_op jit(solution)/shard_map/pallas_call | solution.py:471
  50.2 29.3 %all_to_all.5.back = f32[128,2,128]{2,1,0:T(2,128)} all-to-all(f32[128,2,128]{2,1,0:T(2,128)} %bitcast.4), channel_id=1, replica_groups=mesh['lat'=4,'lon'=32] {'lat','lon'}, dimensions={0} | all-to-all | bytes 262144 | tf_op jit(solution)/shard_map/all_to_all | solution.py:526
  79.4 2.6 %shard_map.124 = f32[96,128]{1,0:T(8,128)} custom-call(s32[2,96]{1,0:T(2,128)} %bitcast.6, s32[96,128]{1,0:T(8,128)} %entry.3, f32[128,2,128]{2,1,0:T(2,128)} %all_to_all.5.back), custom_call_target="tpu_custom_call" | custom-call | tf_op jit(solution)/shard_map/pallas_call | solution.py:500

commit v5 on v4

--- a/solution.py
+++ b/solution.py
@@ -152,17 +152,19 @@
     weight,
     latent_hbm,
     w_hidden,
-    recv,
+    recv_hbm,
     meta,
     left_hbm,
     latent,
     left,
+    recv,
     sent,
     w_t,
     send_sem,
     recv_sem,
     latent_sem,
     left_sem,
+    out_sem,
 ):
     fetch = pltpu.make_async_copy(latent_hbm, latent, latent_sem)
     fetch.start()
@@ -181,7 +183,7 @@
         pl.semaphore_signal(barrier, inc=1, device_id=place(i)[1], device_id_type=mesh_id)
         return c
 
-    lax.fori_loop(1, n_dev, greet, 0)
+    lax.fori_loop(1, n_dev, greet, 0, unroll=4)
     pack(owner, local, entry, offset, frac, value, weight, sent)
     pl.semaphore_wait(barrier, n_dev - 1)
 
@@ -197,7 +199,7 @@
         ).start()
         return c
 
-    lax.fori_loop(1, n_dev, send, 0)
+    lax.fori_loop(1, n_dev, send, 0, unroll=4)
     recv[me] = sent[me]
 
     w_t[...] = w_hidden[...].astype(F32).T.astype(BF16)
@@ -235,20 +237,24 @@
         device_id=place(1)[1],
         device_id_type=mesh_id,
     ).wait()
+    leave_recv = pltpu.make_async_copy(recv.at[:, pl.ds(0, 8), :], recv_hbm, out_sem)
+    leave_recv.start()
     meta[...] = tiling(recv[:, 8, :], n_patch)
+    leave_recv.wait()
     pltpu.make_async_copy(left, left_hbm, left_sem).wait()
 
 
 def compute_kernel(
     meta,
     left_hbm,
-    recv,
+    recv_hbm,
     w_hidden,
     b_hidden,
     w_out,
     grad,
     score,
     left,
+    recv,
     total,
     w_t,
     bias,
@@ -257,6 +263,7 @@
     dense,
     ready,
     left_sem,
+    recv_sem,
     grad_sem,
     *bufs,
 ):
@@ -267,6 +274,8 @@
     lane4 = lax.broadcasted_iota(jnp.int32, (4, 128), 1)
     lane1 = lax.broadcasted_iota(jnp.int32, (1, 128), 1)
 
+    arrive = pltpu.make_async_copy(recv_hbm, recv, recv_sem)
+    arrive.start()
     fetch = pltpu.make_async_copy(left_hbm, left, left_sem)
     fetch.start()
     n_tile = meta[3, 0]
@@ -280,7 +289,7 @@
     def append(i, c):
         for j in range(8):
             s = 8 * i + j
-            rows = recv[s, 0:8, :]
+            rows = recv[s]
             for k in range(2):
                 base, n = meta[0, 128 * k + s], meta[1, 128 * k + s]
                 half, shift = lax.shift_right_logical(base, 7), base & 127
@@ -289,8 +298,6 @@
                 pltpu.store(comp.at[half], turned, mask=(lane4 >= shift) & (lane4 < end))
                 pltpu.store(comp.at[half + 1], turned, mask=lane4 < end - 128)
         return c
-
-    lax.fori_loop(0, n_dev // 8, append, 0)
 
     w_t[...] = w_hidden[...].astype(F32).T.astype(BF16)
     b_parts = three_parts(jnp.broadcast_to(b_hidden[...] * (1.0 / alpha), (128, 256)).T)
@@ -310,6 +317,8 @@
         return c
 
     lax.fori_loop(0, n_patch, clear, 0)
+    arrive.wait()
+    lax.fori_loop(0, n_dev // 8, append, 0)
     fetch.wait()
 
     cells = lax.broadcasted_iota(jnp.int32, (8, 256), 0).astype(F32)
@@ -413,10 +422,8 @@
             p = 4 * i + j
             both = total[p] * (1.5 * head[...])
             high = both.astype(BF16)
-            low = (both - high.astype(F32)).astype(BF16)
             dims = (((0,), (0,)), ((), ()))
             res = lax.dot_general(high, w_t[...], dims, preferred_element_type=F32)
-            res = res + lax.dot_general(low, w_t[...], dims, preferred_element_type=F32)
 
             ready[p, :, 0:256] = res[0:64]
             ready[p, :, 256:512] = res[64:128]
@@ -427,11 +434,51 @@
     pltpu.make_async_copy(ready, grad, grad_sem).wait()
 
 
-def unpack_kernel(owner, entry, back, out):
+def unpack_kernel(owner, entry, score, out, back, send_sem, recv_sem):
+    lat_size, lon_size = lax.axis_size("lat"), lax.axis_size("lon")
+    n_dev = lat_size * lon_size
+    me = lax.axis_index("lat") * lon_size + lax.axis_index("lon")
+    mesh_id = pl.DeviceIdType.MESH
+
+    def place(i):
+        j = lax.rem(me + i, n_dev)
+        return j, (lax.div(j, lon_size), lax.rem(j, lon_size))
+
+    barrier = pltpu.get_barrier_semaphore()
+
+    def greet(i, c):
+        pl.semaphore_signal(barrier, inc=1, device_id=place(i)[1], device_id_type=mesh_id)
+        return c
+
+    lax.fori_loop(1, n_dev, greet, 0, unroll=4)
     sel = selectors(columns(owner[...]))
     where = entry[...]
     lane = lax.broadcasted_iota(jnp.int32, where.shape, 1)
     one = ones_before(where)
+    pl.semaphore_wait(barrier, n_dev - 1)
+
+    def send_one(i, c):
+        j, there = place(i)
+        pltpu.make_async_remote_copy(
+            src_ref=score.at[j],
+            dst_ref=back.at[me],
+            send_sem=send_sem,
+            recv_sem=recv_sem,
+            device_id=there,
+            device_id_type=mesh_id,
+        ).start()
+        return c
+
+    lax.fori_loop(1, n_dev, send_one, 0, unroll=4)
+    back[me] = score[me]
+    pltpu.make_async_remote_copy(
+        src_ref=score.at[pl.ds(0, n_dev - 1)],
+        dst_ref=back.at[pl.ds(0, n_dev - 1)],
+        send_sem=send_sem,
+        recv_sem=recv_sem,
+        device_id=place(1)[1],
+        device_id_type=mesh_id,
+    ).wait()
     got = []
     for e in range(2):
         rows = sum(pick(sel[k][e].astype(BF16), back[:, k, :], ((1,), (0,))) for k in range(2))
@@ -444,17 +491,19 @@
     return pl.pallas_call(
         send_kernel,
         out_shape=(
-            jax.ShapeDtypeStruct((128, 9, 128), F32),
+            jax.ShapeDtypeStruct((128, 8, 128), F32),
             jax.ShapeDtypeStruct((8, 256), jnp.int32),
             jax.ShapeDtypeStruct((n_patch, 512, 128), BF16),
         ),
         in_specs=[VMEM] * 7 + [HBM, VMEM],
-        out_specs=(VMEM, VMEM, HBM),
+        out_specs=(HBM, VMEM, HBM),
         scratch_shapes=[
             pltpu.VMEM(latent.shape, BF16),
             pltpu.VMEM((latent.shape[0], 512, 128), BF16),
             pltpu.VMEM((128, 9, 128), F32),
+            pltpu.VMEM((128, 9, 128), F32),
             pltpu.VMEM((256, 256), BF16),
+            pltpu.SemaphoreType.DMA,
             pltpu.SemaphoreType.DMA,
             pltpu.SemaphoreType.DMA,
             pltpu.SemaphoreType.DMA,
@@ -474,10 +523,11 @@
             jax.ShapeDtypeStruct((n_patch, 64, 512), F32),
             jax.ShapeDtypeStruct((256, 128), F32),
         ),
-        in_specs=[SMEM, HBM] + [VMEM] * 4,
+        in_specs=[SMEM, HBM, HBM] + [VMEM] * 3,
         out_specs=(HBM, VMEM),
         scratch_shapes=[
             pltpu.VMEM(left.shape, BF16),
+            pltpu.VMEM(recv.shape, F32),
             pltpu.VMEM((n_patch, 256, 128), F32),
             pltpu.VMEM((256, 256), BF16),
             pltpu.VMEM((512, 128), BF16),
@@ -487,6 +537,7 @@
             pltpu.VMEM((n_patch, 64, 512), F32),
             pltpu.SemaphoreType.DMA,
             pltpu.SemaphoreType.DMA,
+            pltpu.SemaphoreType.DMA,
         ]
         + [pltpu.VMEM((512, 256), BF16)] * UNROLL
         + [pltpu.VMEM((512, 256), F32)] * UNROLL
@@ -496,14 +547,21 @@
     )(meta, left, recv, w_hidden, b_hidden.reshape(1, 256), w_out)
 
 
-def unpack(patch_owner, obs_patch, back):
+def unpack(patch_owner, obs_patch, score):
     return pl.pallas_call(
         unpack_kernel,
         out_shape=jax.ShapeDtypeStruct(obs_patch.shape, F32),
         in_specs=[VMEM] * 3,
         out_specs=VMEM,
-        compiler_params=pltpu.CompilerParams(vmem_limit_bytes=60 * 1024 * 1024),
-    )(patch_owner, obs_patch, back)
+        scratch_shapes=[
+            pltpu.VMEM(score.shape, F32),
+            pltpu.SemaphoreType.DMA,
+            pltpu.SemaphoreType.DMA,
+        ],
+        compiler_params=pltpu.CompilerParams(
+            vmem_limit_bytes=60 * 1024 * 1024, collective_id=1, has_side_effects=True
+        ),
+    )(patch_owner, obs_patch, score)
 
 
 def per_device(
@@ -523,8 +581,7 @@
         patch_owner.T, patch_local.T, obs_patch, cell_offset, frac, obs_value, obs_weight, latent, w_hidden
     )
     grad, score = compute(meta, left, recv, w_hidden, b_hidden, w_out)
-    back = lax.all_to_all(score.reshape(128, 2, 128), AXES, 0, 0, tiled=True)
-    return (grad, unpack(patch_owner.T, obs_patch, back))
+    return (grad, unpack(patch_owner.T, obs_patch, score.reshape(128, 2, 128)))
 
 
 def solution(mesh):

time: 82.3 us -> 77.1 us (0.937)
  blocking collectives: 29.3 us -> 0 us
  Pallas kernels: 52.2 us -> 74.8 us
  local copies, waits for them, and re-layouts: 0 us -> 1.42 us
    all_to_all x1 -> x0, blocking collectives: 29.3 us -> none  [per_device(): back = lax.all_to_all(score.reshape(128, 2, 128), AXES, 0, 0, tiled=True)]
    pallas_call x1, Pallas kernels: 2.63 us -> 26.3 us  [unpack(): pl.pallas_call(unpack_kernel, out_shape=jax.ShapeDtypeStruct(obs_patch.sh...]
    unnamed x0 -> x1, local copies, waits for them, and re-layouts: none -> 1.42 us
where the time goes in v5:
time: 77.1 us; the launch traced here: 76.9 us
  Pallas kernels  74.8 us (97%)
  local copies, waits for them, and re-layouts  1.42 us (2%)
    pallas_call x1, Pallas kernels, unpack(): pl.pallas_call(unpack_kernel, out_shape=jax.ShapeDtypeStruct(obs_patch.sh...  26.3 us
    pallas_call x1, Pallas kernels, compute(): pl.pallas_call(compute_kernel, out_shape=(jax.ShapeDtypeStruct((n_patch,...  26.1 us
    pallas_call x1, Pallas kernels, send(): pl.pallas_call(send_kernel, out_shape=(jax.ShapeDtypeStruct((128, 8, 128)...  22.4 us

profile of v5, /device:TPU:1, one launch (start us, length us, event | category | flops | bytes accessed | tf_op | source)
XLA Modules:
  0.0 76.9 jit_solution(15509202336816987538)
XLA Ops:
  0.6 22.4 %shard_map.122 = (f32[128,8,128]{2,1,0:T(8,128)}, s32[8,256]{1,0:T(8,128)}, bf16[32,512,128]{2,1,0:T(8,128)(2,1)}) custom-call(s32[2,96]{1,0:T(2,128)} %bitcast.5, s32[2,96]{1,0:T(2,128)} %bitcast.7, s32[96,128]{1,0:T(8,128)} %entry.3, s32[96,128]{1,0:T(8,128)} %offset.1, f32[96,2,128]{2,1,0:T(2,128)} %frac.1, f32[96,128]{1,0:T(8,128)} %value.1, ...), custom_call_target="tpu_custom_call" | custom-call | tf_op jit(solution)/shard_map/pallas_call | solution.py:491
  23.1 26.1 %shard_map.123 = (f32[32,64,512]{2,1,0:T(8,128)}, f32[256,128]{1,0:T(8,128)}) custom-call(s32[8,256]{1,0:T(8,128)} %get-tuple-element.7.meta, bf16[32,512,128]{2,1,0:T(8,128)(2,1)} %get-tuple-element.8.left_hbm, f32[128,8,128]{2,1,0:T(8,128)} %get-tuple-element.9.recv_hbm, bf16[256,256]{1,0:T(8,128)(2,1)} %w_hidden.3, f32[1,256]{1,0:T(1,128)} %bitcast.8, ...), custom_call_target="tpu_custom_call" | custom-call | tf_op jit(solution)/shard_map/pallas_call | solution.py:520
  49.2 26.3 %shard_map.124 = f32[96,128]{1,0:T(8,128)} custom-call(s32[2,96]{1,0:T(2,128)} %bitcast.6, s32[96,128]{1,0:T(8,128)} %entry.3, f32[128,2,128]{2,1,0:T(2,128)} %bitcast.4), custom_call_target="tpu_custom_call" | custom-call | tf_op jit(solution)/shard_map/pallas_call | solution.py:551
  75.5 1.4 %copy.14 = f32[96,128]{1,0:T(8,128)} copy(f32[96,128]{1,0:T(8,128)} %shard_map.124) | data formatting | bytes 98304

commit v6 on v5

--- a/solution.py
+++ b/solution.py
@@ -418,8 +418,8 @@
         return pltpu.make_async_copy(ready.at[p], grad.at[p], grad_sem)
 
     def finish(i, c):
-        for j in range(4):
-            p = 4 * i + j
+        for j in range(8):
+            p = 8 * i + j
             both = total[p] * (1.5 * head[...])
             high = both.astype(BF16)
             dims = (((0,), (0,)), ((), ()))
@@ -430,7 +430,7 @@
             leave(p).start()
         return c
 
-    lax.fori_loop(0, n_patch // 4, finish, 0)
+    lax.fori_loop(0, n_patch // 8, finish, 0)
     pltpu.make_async_copy(ready, grad, grad_sem).wait()
 
 

time: 77.1 us -> 76.6 us (level)
    pallas_call x1, Pallas kernels: 26.3 us -> 14.7 us  [unpack(): pl.pallas_call(unpack_kernel, out_shape=jax.ShapeDtypeStruct(obs_patch.sh...]
    pallas_call x1, Pallas kernels: 26.1 us -> 37.2 us  [compute(): pl.pallas_call(compute_kernel, out_shape=(jax.ShapeDtypeStruct((n_patch,...]
where the time goes in v6:
time: 76.6 us; the launch traced here: 76.3 us
  Pallas kernels  74.3 us (97%)
  local copies, waits for them, and re-layouts  1.42 us (2%)
    pallas_call x1, Pallas kernels, compute(): pl.pallas_call(compute_kernel, out_shape=(jax.ShapeDtypeStruct((n_patch,...  37.2 us
    pallas_call x1, Pallas kernels, send(): pl.pallas_call(send_kernel, out_shape=(jax.ShapeDtypeStruct((128, 8, 128)...  22.4 us
    pallas_call x1, Pallas kernels, unpack(): pl.pallas_call(unpack_kernel, out_shape=jax.ShapeDtypeStruct(obs_patch.sh...  14.7 us

profile of v6, /device:TPU:1, one launch (start us, length us, event | category | flops | bytes accessed | tf_op | source)
XLA Modules:
  0.0 76.3 jit_solution(6738611673353586720)
XLA Ops:
  0.6 22.4 %shard_map.122 = (f32[128,8,128]{2,1,0:T(8,128)}, s32[8,256]{1,0:T(8,128)}, bf16[32,512,128]{2,1,0:T(8,128)(2,1)}) custom-call(s32[2,96]{1,0:T(2,128)} %bitcast.5, s32[2,96]{1,0:T(2,128)} %bitcast.7, s32[96,128]{1,0:T(8,128)} %entry.3, s32[96,128]{1,0:T(8,128)} %offset.1, f32[96,2,128]{2,1,0:T(2,128)} %frac.1, f32[96,128]{1,0:T(8,128)} %value.1, ...), custom_call_target="tpu_custom_call" | custom-call | tf_op jit(solution)/shard_map/pallas_call | solution.py:491
  23.1 37.2 %shard_map.123 = (f32[32,64,512]{2,1,0:T(8,128)}, f32[256,128]{1,0:T(8,128)}) custom-call(s32[8,256]{1,0:T(8,128)} %get-tuple-element.7.meta, bf16[32,512,128]{2,1,0:T(8,128)(2,1)} %get-tuple-element.8.left_hbm, f32[128,8,128]{2,1,0:T(8,128)} %get-tuple-element.9.recv_hbm, bf16[256,256]{1,0:T(8,128)(2,1)} %w_hidden.3, f32[1,256]{1,0:T(1,128)} %bitcast.8, ...), custom_call_target="tpu_custom_call" | custom-call | tf_op jit(solution)/shard_map/pallas_call | solution.py:520
  60.2 14.7 %shard_map.124 = f32[96,128]{1,0:T(8,128)} custom-call(s32[2,96]{1,0:T(2,128)} %bitcast.6, s32[96,128]{1,0:T(8,128)} %entry.3, f32[128,2,128]{2,1,0:T(2,128)} %bitcast.4), custom_call_target="tpu_custom_call" | custom-call | tf_op jit(solution)/shard_map/pallas_call | solution.py:551
  74.9 1.4 %copy.14 = f32[96,128]{1,0:T(8,128)} copy(f32[96,128]{1,0:T(8,128)} %shard_map.124) | data formatting | bytes 98304

commit v7 on v6

--- a/solution.py
+++ b/solution.py
@@ -418,8 +418,8 @@
         return pltpu.make_async_copy(ready.at[p], grad.at[p], grad_sem)
 
     def finish(i, c):
-        for j in range(8):
-            p = 8 * i + j
+        for j in range(16):
+            p = 16 * i + j
             both = total[p] * (1.5 * head[...])
             high = both.astype(BF16)
             dims = (((0,), (0,)), ((), ()))
@@ -430,7 +430,7 @@
             leave(p).start()
         return c
 
-    lax.fori_loop(0, n_patch // 8, finish, 0)
+    lax.fori_loop(0, n_patch // 16, finish, 0)
     pltpu.make_async_copy(ready, grad, grad_sem).wait()
 
 

time: 76.6 us -> 76.5 us (level)
    pallas_call x1, Pallas kernels: 14.7 us -> 26.6 us  [unpack(): pl.pallas_call(unpack_kernel, out_shape=jax.ShapeDtypeStruct(obs_patch.sh...]
    pallas_call x1, Pallas kernels: 37.2 us -> 25.4 us  [compute(): pl.pallas_call(compute_kernel, out_shape=(jax.ShapeDtypeStruct((n_patch,...]
where the time goes in v7:
time: 76.5 us
  Pallas kernels  74.4 us (97%)
  local copies, waits for them, and re-layouts  1.42 us (2%)
    pallas_call x1, Pallas kernels, unpack(): pl.pallas_call(unpack_kernel, out_shape=jax.ShapeDtypeStruct(obs_patch.sh...  26.6 us
    pallas_call x1, Pallas kernels, compute(): pl.pallas_call(compute_kernel, out_shape=(jax.ShapeDtypeStruct((n_patch,...  25.4 us
    pallas_call x1, Pallas kernels, send(): pl.pallas_call(send_kernel, out_shape=(jax.ShapeDtypeStruct((128, 8, 128)...  22.4 us

profile of v7, /device:TPU:1, one launch (start us, length us, event | category | flops | bytes accessed | tf_op | source)
XLA Modules:
  0.0 76.5 jit_solution(17979704141905582480)
XLA Ops:
  0.6 22.4 %shard_map.122 = (f32[128,8,128]{2,1,0:T(8,128)}, s32[8,256]{1,0:T(8,128)}, bf16[32,512,128]{2,1,0:T(8,128)(2,1)}) custom-call(s32[2,96]{1,0:T(2,128)} %bitcast.5, s32[2,96]{1,0:T(2,128)} %bitcast.7, s32[96,128]{1,0:T(8,128)} %entry.3, s32[96,128]{1,0:T(8,128)} %offset.1, f32[96,2,128]{2,1,0:T(2,128)} %frac.1, f32[96,128]{1,0:T(8,128)} %value.1, ...), custom_call_target="tpu_custom_call" | custom-call | tf_op jit(solution)/shard_map/pallas_call | solution.py:491
  23.1 25.4 %shard_map.123 = (f32[32,64,512]{2,1,0:T(8,128)}, f32[256,128]{1,0:T(8,128)}) custom-call(s32[8,256]{1,0:T(8,128)} %get-tuple-element.7.meta, bf16[32,512,128]{2,1,0:T(8,128)(2,1)} %get-tuple-element.8.left_hbm, f32[128,8,128]{2,1,0:T(8,128)} %get-tuple-element.9.recv_hbm, bf16[256,256]{1,0:T(8,128)(2,1)} %w_hidden.3, f32[1,256]{1,0:T(1,128)} %bitcast.8, ...), custom_call_target="tpu_custom_call" | custom-call | tf_op jit(solution)/shard_map/pallas_call | solution.py:520
  48.5 26.6 %shard_map.124 = f32[96,128]{1,0:T(8,128)} custom-call(s32[2,96]{1,0:T(2,128)} %bitcast.6, s32[96,128]{1,0:T(8,128)} %entry.3, f32[128,2,128]{2,1,0:T(2,128)} %bitcast.4), custom_call_target="tpu_custom_call" | custom-call | tf_op jit(solution)/shard_map/pallas_call | solution.py:551
  75.1 1.4 %copy.14 = f32[96,128]{1,0:T(8,128)} copy(f32[96,128]{1,0:T(8,128)} %shard_map.124) | data formatting | bytes 98304
